TPU v7x, 512 devices: a whole 4x4x16 slice. The times are simulated.
512 devices in a mesh: ctx: 64 (over z_lo, x, core), mem: 8 (over z_hi, y).
Axes of the slice: x: 4, y: 4, z: 16 (z_hi: 2, z_lo: 8; z = z_hi * 8 + z_lo), core: 2. Of those that a mesh axis runs over, the one named last changes fastest.
Arguments:
- queries: bfloat16 [16384, 4096], P('ctx', 'mem'), may hold values from -5 to 5
- keys: bfloat16 [16384, 4096], P('ctx', 'mem'), may hold values from -5 to 5
- values: bfloat16 [16384, 4096], P('ctx', 'mem'), may hold values from -400 to 400
- memory_keys: bfloat16 [512, 64, 4096], P('ctx', None, 'mem'), may hold values from -5 to 5
- memory_values: bfloat16 [512, 64, 4096], P('ctx', None, 'mem'), may hold values from -400 to 400
- retrieval: int32 [128, 4], P('ctx'), may hold values from 0 to 511, as said below
- gate: float32 [32], P('mem'), may hold values from -2 to 2
- gain: float32 [4096], P('mem'), may hold values from 0.5 to 2
Outputs:
- attended: bfloat16 [16384, 4096], P('ctx', 'mem')
Inputs may be any that keep to these rules, and one draw needn't show every extreme that they name: `retrieval`: block b belongs to owner b // 8. Among the 8 ids of the 2 tiles of one index of ctx, no owner is named more than once. There is one owner (the same for all) that every index of ctx names exactly once. The 4 ids of a tile differ.
All inputs are finite; a program needn't handle non-finite values.
Results may differ from a plain program's by a relative error of at most 0.015.
Values may be sent and summed in bfloat16 or wider, within the bound.
A program may use at most 128 MiB of HBM per device.

v0:
```python
import math

import jax
import jax.numpy as jnp
from jax import lax
from jax.sharding import PartitionSpec as P

HEADS = 32
HEAD_DIM = 128
MBLK_DEV = 8
QTILE = 128
MBLOCK = 64
TOPK = 4
SPAN = 2


def passed_along(block, axis, distance):
    devices = range(lax.axis_size(axis))
    route = [(i - distance, i) for i in devices if i - distance in devices]
    return lax.ppermute(block, axis, route)


def window_attention(queries, near_keys, near_values, first_query, first_key, head_count, window):
    query_rows = queries.shape[0]
    key_rows = near_keys.shape[0]
    query_pos = first_query + jnp.arange(query_rows, dtype=jnp.int32)
    key_pos = first_key + jnp.arange(key_rows, dtype=jnp.int32)
    offsets = query_pos[:, None] - key_pos[None, :]
    allowed = (offsets >= 0) & (offsets < window) & (key_pos >= 0)[None, :]
    score_scale = 1.0 / math.sqrt(HEAD_DIM)
    head_outputs = []
    for head_index in range(head_count):
        column = head_index * HEAD_DIM
        query_heads = queries[:, column : column + HEAD_DIM]
        key_heads = near_keys[:, column : column + HEAD_DIM]
        value_heads = near_values[:, column : column + HEAD_DIM]
        scores = jnp.dot(query_heads, key_heads.T, preferred_element_type=jnp.float32) * score_scale
        scores = jnp.where(allowed, scores, -jnp.inf)
        row_peak = jnp.max(scores, axis=1, keepdims=True)
        weights = jnp.exp(scores - row_peak)
        row_total = jnp.sum(weights, axis=1, keepdims=True)
        product = jnp.dot(
            weights.astype(jnp.bfloat16), value_heads, preferred_element_type=jnp.float32
        )
        head_outputs.append(product / row_total)
    return jnp.concatenate(head_outputs, axis=1)


def block_partial(tile_queries, block_keys, block_values, head_count):
    leading = tile_queries.shape[:-2]
    query_rows = tile_queries.shape[-2]
    key_rows = block_keys.shape[-2]
    query_heads = tile_queries.reshape(leading + (query_rows, head_count, HEAD_DIM))
    key_heads = block_keys.reshape(leading + (key_rows, head_count, HEAD_DIM))
    value_heads = block_values.reshape(leading + (key_rows, head_count, HEAD_DIM))
    score_scale = 1.0 / math.sqrt(HEAD_DIM)
    scores = (
        jnp.einsum(
            "...qhd,...khd->...hqk", query_heads, key_heads, preferred_element_type=jnp.float32
        )
        * score_scale
    )
    block_peak = jnp.max(scores, axis=-1)
    weights = jnp.exp(scores - block_peak[..., None])
    block_total = jnp.sum(weights, axis=-1)
    product = jnp.einsum(
        "...hqk,...khd->...qhd",
        weights.astype(jnp.bfloat16),
        value_heads,
        preferred_element_type=jnp.float32,
    )
    product = product / jnp.swapaxes(block_total, -1, -2)[..., None]
    return (
        product.astype(jnp.bfloat16).reshape(leading + (query_rows, head_count * HEAD_DIM)),
        block_peak,
        block_total,
    )


def combine_blocks(block_out, block_peak, block_total, head_count):
    tile_peak = jnp.max(block_peak, axis=1, keepdims=True)
    mix_weight = block_total * jnp.exp(block_peak - tile_peak)
    mix_total = jnp.sum(mix_weight, axis=1)
    tiles, blocks, query_rows = (block_out.shape[0], block_out.shape[1], block_out.shape[2])
    outputs = block_out.astype(jnp.float32).reshape(tiles, blocks, query_rows, head_count, HEAD_DIM)
    summed = jnp.sum(jnp.swapaxes(mix_weight, -1, -2)[..., None] * outputs, axis=1)
    mixed = summed / jnp.swapaxes(mix_total, -1, -2)[..., None]
    return mixed.reshape(tiles * query_rows, head_count * HEAD_DIM)


def shards(queries, keys, values, memory_keys, memory_values, retrieval, gate, gain):
    rows_here, feature_width = queries.shape
    heads_here = feature_width // HEAD_DIM
    owners = lax.axis_size("ctx")
    cycle_index = lax.axis_index("ctx")
    tiles = rows_here // QTILE
    requests = tiles * TOPK
    capacity = max(1, 2 * requests // owners)
    pieces = []
    current = (keys, values)
    for distance in range(SPAN):
        current = passed_along((current[0], current[1]), "ctx", 1)
        pieces.insert(0, current)
    near_keys = jnp.concatenate([piece[0] for piece in pieces] + [keys], axis=0)
    near_values = jnp.concatenate([piece[1] for piece in pieces] + [values], axis=0)
    window = SPAN * rows_here
    first_query = cycle_index * rows_here
    first_key = first_query - window
    local_parts = window_attention(
        queries, near_keys, near_values, first_query + 0, first_key + 0, heads_here, window
    )
    flat_ids = retrieval.reshape(requests)
    owner_ids = flat_ids // MBLK_DEV
    picked = flat_ids % MBLK_DEV
    request_order = jnp.arange(requests, dtype=jnp.int32)
    same_owner = owner_ids[:, None] == owner_ids[None, :]
    rank_within = jnp.sum(same_owner & (request_order[None, :] < request_order[:, None]), axis=1)
    slot_index = owner_ids * capacity + rank_within
    slot_table = (
        slot_index[:, None] == jnp.arange(owners * capacity, dtype=jnp.int32)[None, :]
    ).astype(jnp.int32)
    send_ids = jnp.sum(slot_table * (picked + 1)[:, None], axis=0).reshape(owners, capacity)
    tile_queries = queries.reshape(tiles, QTILE, feature_width)
    slot_ids = lax.all_to_all(send_ids, "ctx", split_axis=0, concat_axis=0, tiled=True)
    chosen = jnp.maximum(slot_ids - 1, 0)
    occupied = (slot_ids > 0)[..., None, None]
    found_keys = jnp.where(occupied, memory_keys[chosen], 0)
    found_values = jnp.where(occupied, memory_values[chosen], 0)
    got_keys = lax.all_to_all(found_keys, "ctx", split_axis=0, concat_axis=0, tiled=True)
    got_values = lax.all_to_all(found_values, "ctx", split_axis=0, concat_axis=0, tiled=True)
    got_keys = got_keys.reshape(owners * capacity, MBLOCK, feature_width)[slot_index]
    got_values = got_values.reshape(owners * capacity, MBLOCK, feature_width)[slot_index]
    got_keys = got_keys.reshape(tiles, TOPK, MBLOCK, feature_width)
    got_values = got_values.reshape(tiles, TOPK, MBLOCK, feature_width)
    expanded = jnp.broadcast_to(tile_queries[:, None], (tiles, TOPK, QTILE, feature_width))
    block_out, block_peak, block_total = block_partial(expanded, got_keys, got_values, heads_here)
    memory_out = combine_blocks(block_out, block_peak, block_total, heads_here)
    factor = jnp.repeat(jax.nn.sigmoid(gate), HEAD_DIM)
    combined = factor * memory_out + (1.0 - factor) * local_parts
    square_sum = lax.psum(jnp.sum(combined * combined, axis=1), "mem")
    return (combined * gain * lax.rsqrt(square_sum[:, None] / (HEADS * HEAD_DIM) + 1e-06)).astype(
        jnp.bfloat16
    )


def solution(mesh):
    in_specs = (
        P("ctx", "mem"),
        P("ctx", "mem"),
        P("ctx", "mem"),
        P("ctx", None, "mem"),
        P("ctx", None, "mem"),
        P("ctx", None),
        P("mem"),
        P("mem"),
    )
    out_specs = P("ctx", "mem")
    return jax.shard_map(shards, mesh=mesh, in_specs=in_specs, out_specs=out_specs, check_vma=False)
```

profile of v0, /device:TPU:128, one launch (start us, length us, event | category | flops | bytes accessed | tf_op | source)
XLA Modules:
  0.0 495.3 jit_solution(2757061282309150296)
XLA Ops:
  0.0 0.0 copy-start
  0.0 0.8 reshape.285
  0.8 0.2 convert_reduce_fusion
  1.0 0.1 select_reduce_fusion
  1.1 0.1 copy.25
  1.2 21.5 %all_to_all.19 = s32[64,1,1]{2,1,0:T(1,128)S(1)} all-to-all(s32[64,1,1]{2,1,0:T(1,128)S(1)} %copy.25), channel_id=1, replica_groups=mesh['ctx'=64,'mem'=8] {'ctx'}, dimensions={0} | all-to-all | bytes 512 | tf_op jit(solution)/shard_map/all_to_all | solution.py:124
  22.7 1.2 maximum_reduce_fusion
  23.9 0.0 copy-done
  23.9 0.0 copy-start.1
  24.0 2.7 gather_fusion
  26.7 0.0 copy-done.1
  26.7 2.8 gather_fusion.2
  29.5 1.2 compare_reduce_fusion
  30.7 5.1 %bitcast_select_fusion = (bf16[64,1,64,512]{3,2,1,0:T(8,128)(2,1)}, bf16[64,1,64,512]{3,2,1,0:T(8,128)(2,1)S(1)}) fusion(bf16[64,64,512]{2,1,0:T(8,128)(2,1)} %gather_fusion.2, pred[64]{0:T(512)(128)(4,1)S(1)} %compare_reduce_fusion, bf16[64,64,512]{2,1,0:T(8,128)(2,1)} %gather_fusion), kind=kLoop, calls=%fused_computation.4 | loop fusion | flops 4194304 | bytes 16777280 | tf_op jit(solution)/shard_map/jit(_where)/select_n | solution.py:128
  35.9 190.6 %all_to_all.20 = bf16[64,1,64,512]{3,2,1,0:T(8,128)(2,1)} all-to-all(bf16[64,1,64,512]{3,2,1,0:T(8,128)(2,1)S(1)} %get-tuple-element.10), channel_id=1, replica_groups=mesh['ctx'=64,'mem'=8] {'ctx'}, dimensions={0} | all-to-all | bytes 8388608 | tf_op jit(solution)/shard_map/all_to_all | solution.py:129
  226.5 0.0 copy-start.2
  226.5 0.0 copy-start.3
  226.5 0.0 copy-start.6
  226.5 0.0 copy-start.4
  226.5 13.5 %all-to-all-start.2 = ((bf16[64,1,64,512]{3,2,1,0:T(8,128)(2,1)}), bf16[64,1,64,512]{3,2,1,0:T(8,128)(2,1)}, u32[]{:S(2)}, u32[]{:S(2)}) async-start(bf16[64,1,64,512]{3,2,1,0:T(8,128)(2,1)} %get-tuple-element.9), calls=%async_computation.2 | async-start | bytes 8388608 | tf_op jit(solution)/shard_map/all_to_all | solution.py:130
  240.0 0.0 copy-done.2
  240.0 2.1 collective-permute-start
  242.1 0.0 copy-done.3
  242.1 3.4 collective-permute-start.2
  245.5 0.0 copy-done.6
  245.5 0.1 reshape.287
  245.6 0.0 copy-done.7
  245.6 0.1 bitcast_subtract_fusion.1
  245.7 180.5 %collective-permute-done = bf16[256,512]{1,0:T(8,128)(2,1)S(1)} collective-permute-done((bf16[256,512]{1,0:T(8,128)(2,1)S(1)}, bf16[256,512]{1,0:T(8,128)(2,1)S(1)}, u32[]{:S(2)}, u32[]{:S(2)}) %collective-permute-start) | collective-permute-done | bytes 262176 | tf_op jit(solution)/shard_map/ppermute | solution.py:20
  426.2 1.9 collective-permute-start.1
  428.1 0.0 copy-done.4
  428.1 0.1 broadcast_in_dim.32
  428.3 0.1 broadcast_bitcast_fusion
  428.3 0.7 collective-permute-done.2
  429.0 1.9 collective-permute-start.3
  430.9 6.3 %collective-permute-done.1 = bf16[256,512]{1,0:T(8,128)(2,1)S(1)} collective-permute-done((bf16[256,512]{1,0:T(8,128)(2,1)S(1)}, bf16[256,512]{1,0:T(8,128)(2,1)S(1)}, u32[]{:S(2)}, u32[]{:S(2)}) %collective-permute-start.1) | collective-permute-done | bytes 262176 | tf_op jit(solution)/shard_map/ppermute | solution.py:20
  437.3 2.8 collective-permute-done.3
  440.2 0.4 fusion.53
  440.6 0.2 fusion.20
  440.8 0.4 fusion.54
  441.2 0.2 fusion.18
  441.4 0.4 fusion.55
  441.8 0.2 fusion.16
  441.9 0.4 fusion.56
  442.3 0.2 fusion.14
  442.5 0.3 convolution_divide_fusion
  442.8 0.3 convolution_divide_fusion.1
  443.1 0.3 convolution_divide_fusion.2
  443.4 0.3 convolution_divide_fusion.3
  443.7 2.8 gather_fusion.1
  446.4 0.1 reshape_reshape.6
  446.6 0.8 fusion.52
  447.4 0.2 fusion.11
  447.7 0.0 all-to-all-done.2
  447.7 2.8 gather_fusion.3
  450.5 0.1 reshape_reshape.7
  450.6 0.0 copy-start.5
  450.6 0.6 multiply_reduce_fusion
  451.3 0.4 copy.29
  451.7 0.2 multiply_reduce_fusion.1
  451.9 42.3 %psum.7 = f32[256]{0:T(256)S(1)} all-reduce(f32[256]{0:T(256)S(1)} %multiply_reduce_fusion.1), channel_id=1, replica_groups=mesh['ctx'=64,'mem'=8] {'mem'}, use_global_device_ids=true, to_apply=%region_16.17 | all-reduce | flops 256 | bytes 2048 | tf_op jit(solution)/shard_map/psum | solution.py:140
  494.2 0.0 copy-done.5
  494.2 0.3 multiply_convert_fusion
  494.5 0.8 copy.30
  (21 shorter events, 0.3 us)
Async XLA Ops:
  0.0 23.9 %copy-start = (bf16[8,64,512]{2,1,0:T(8,128)(2,1)S(1)}, bf16[8,64,512]{2,1,0:T(8,128)(2,1)}, u32[]{:S(2)}) copy-start(bf16[8,64,512]{2,1,0:T(8,128)(2,1)} %param.11) | copy-start | bytes 1572868
  23.9 2.8 copy-start.1
  226.5 13.5 %copy-start.2 = (bf16[256,512]{1,0:T(8,128)(2,1)S(1)}, bf16[256,512]{1,0:T(8,128)(2,1)}, u32[]{:S(2)}) copy-start(bf16[256,512]{1,0:T(8,128)(2,1)} %param.9) | copy-start | bytes 786436
  226.5 15.6 %copy-start.3 = (bf16[256,512]{1,0:T(8,128)(2,1)S(1)}, bf16[256,512]{1,0:T(8,128)(2,1)}, u32[]{:S(2)}) copy-start(bf16[256,512]{1,0:T(8,128)(2,1)} %param.10) | copy-start | bytes 786436
  226.5 19.0 %copy-start.6 = (s32[2,4]{1,0:T(2,128)S(1)}, s32[2,4]{1,0:T(2,128)}, u32[]{:S(2)}) copy-start(s32[2,4]{1,0:T(2,128)} %param.13) | copy-start | bytes 100
  226.5 19.1 %copy-start.7 = (f32[4]{0:T(128)S(1)}, f32[4]{0:T(128)}, u32[]{:S(2)}) copy-start(f32[4]{0:T(128)} %param.14) | copy-start | bytes 52
  226.5 201.6 %copy-start.4 = (bf16[256,512]{1,0:T(8,128)(2,1)S(1)}, bf16[256,512]{1,0:T(8,128)(2,1)}, u32[]{:S(2)}) copy-start(bf16[256,512]{1,0:T(8,128)(2,1)} %param.8) | copy-start | bytes 786436
  226.5 221.2 %all-to-all-start.2 = ((bf16[64,1,64,512]{3,2,1,0:T(8,128)(2,1)}), bf16[64,1,64,512]{3,2,1,0:T(8,128)(2,1)}, u32[]{:S(2)}, u32[]{:S(2)}) async-start(bf16[64,1,64,512]{3,2,1,0:T(8,128)(2,1)} %get-tuple-element.9), calls=%async_computation.2 | async-start | bytes 8388608 | tf_op jit(solution)/shard_map/all_to_all | solution.py:130
  240.0 186.2 %collective-permute-start = (bf16[256,512]{1,0:T(8,128)(2,1)S(1)}, bf16[256,512]{1,0:T(8,128)(2,1)S(1)}, u32[]{:S(2)}, u32[]{:S(2)}) collective-permute-start(bf16[256,512]{1,0:T(8,128)(2,1)S(1)} %copy-done.2), channel_id=1, source_target_pairs={{0,8},{8,16},{16,24},{24,32},{32,40},{40,48},{48,56},{56,64},{64,7... | collective-permute-start | bytes 786440 | tf_op jit(solution)/shard_map/ppermute | solution.py:20
  242.1 186.9 %collective-permute-start.2 = (bf16[256,512]{1,0:T(8,128)(2,1)S(1)}, bf16[256,512]{1,0:T(8,128)(2,1)S(1)}, u32[]{:S(2)}, u32[]{:S(2)}) collective-permute-start(bf16[256,512]{1,0:T(8,128)(2,1)S(1)} %copy-done.3), channel_id=1, source_target_pairs={{0,8},{8,16},{16,24},{24,32},{32,40},{40,48},{48,56},{56,64},{64,7... | collective-permute-start | bytes 786440 | tf_op jit(solution)/shard_map/ppermute | solution.py:20
  426.2 11.0 %collective-permute-start.1 = (bf16[256,512]{1,0:T(8,128)(2,1)S(1)}, bf16[256,512]{1,0:T(8,128)(2,1)S(1)}, u32[]{:S(2)}, u32[]{:S(2)}) collective-permute-start(bf16[256,512]{1,0:T(8,128)(2,1)S(1)} %collective-permute-done), channel_id=1, source_target_pairs={{0,8},{8,16},{16,24},{24,32},{32,40},{40,48},{48,56},{56,64},{64,7... | collective-permute-start | bytes 786440 | tf_op jit(solution)/shard_map/ppermute | solution.py:20
  429.0 11.1 %collective-permute-start.3 = (bf16[256,512]{1,0:T(8,128)(2,1)S(1)}, bf16[256,512]{1,0:T(8,128)(2,1)S(1)}, u32[]{:S(2)}, u32[]{:S(2)}) collective-permute-start(bf16[256,512]{1,0:T(8,128)(2,1)S(1)} %collective-permute-done.2), channel_id=1, source_target_pairs={{0,8},{8,16},{16,24},{24,32},{32,40},{40,48},{48,56},{56,64},{64,7... | collective-permute-start | bytes 786440 | tf_op jit(solution)/shard_map/ppermute | solution.py:20
  450.6 43.6 %copy-start.5 = (f32[512]{0:T(512)S(1)}, f32[512]{0:T(512)}, u32[]{:S(2)}) copy-start(f32[512]{0:T(512)} %param.15) | copy-start | bytes 6148
where the time goes:
time: 496 us; the launch traced here: 495 us
  blocking collectives  254 us (51%)
  waiting for transfers between devices  190 us (38%)
  starting transfers between devices  22.7 us (5%)
  local copies, waits for them, and re-layouts  13.9 us (3%)
  other arithmetic  9.54 us (2%)
    all_to_all x1, blocking collectives, shards(): lax.all_to_all(found_keys, 'ctx', split_axis=0, concat_axis=0, tiled=True)  191 us
    ppermute x4, waiting for transfers between devices, passed_along(): return lax.ppermute(block, axis, route)  190 us
    psum x1, blocking collectives, shards(): square_sum = lax.psum(jnp.sum(combined * combined, axis=1), 'mem')  42.3 us
    all_to_all x1, blocking collectives, shards(): lax.all_to_all(send_ids, 'ctx', split_axis=0, concat_axis=0, tiled=True)  21.5 us
    all_to_all x1, starting transfers between devices, shards(): lax.all_to_all(found_values, 'ctx', split_axis=0, concat_axis=0, tiled=True)  13.5 us
  transfers between devices with their start and end apart: 5, of which 4 were waited for; matrix products, arithmetic and copies ran while one was open for 2% of the time, Pallas kernels for 0%

commit v1 on v0

v1 whole, which is shorter than its diff:
```python
import functools
import math

import jax
import jax.numpy as jnp
from jax import lax
from jax.experimental import pallas as pl
from jax.experimental.pallas import tpu as pltpu
from jax.sharding import PartitionSpec as P

MESH = pl.DeviceIdType.MESH
ANY = pl.BlockSpec(memory_space=pl.ANY)
VMEM = pl.BlockSpec(memory_space=pltpu.VMEM)
SMEM = pl.BlockSpec(memory_space=pltpu.SMEM)
F32 = jnp.float32
BF16 = jnp.bfloat16

HD = 128
HEADS_HERE = 4
FEATURES = 4096
PLANES = 8
PLANE = 8
REQ = 8
BLK = 64
LOCAL = 64
SLOTS = 256
TOK = 256
CHUNKS = 2
ROWS = BLK // CHUNKS
SCALE = 1.0 / math.sqrt(HD)

SHORT_CAPS = (56, 88, 112, 120)
LONG_CAPS = (64, 128, 192, 256)


def iota(shape, dim):
    return lax.broadcasted_iota(jnp.int32, shape, dim).astype(F32)


def greet(peers):
    barrier = pltpu.get_barrier_semaphore()
    total = 0
    for device, present in peers:
        if present is None:
            pl.semaphore_signal(barrier, inc=1, device_id=device, device_id_type=MESH)
            total = total + 1
        else:

            @pl.when(present)
            def _(device=device):
                pl.semaphore_signal(barrier, inc=1, device_id=device, device_id_type=MESH)

            total = total + present.astype(jnp.int32)
    pl.semaphore_wait(barrier, total)


def schedule(lists, my_z, table_ref):
    block = iota((1, PLANES * LOCAL), 1)
    asker_z = jnp.floor(iota((PLANES * PLANE, 1), 0) / PLANE)
    top = jnp.full((1, PLANES * LOCAL), -1.0, F32)
    low = jnp.full((1, PLANES * LOCAL), 8.0, F32)
    for j in range(REQ):
        hit = lists[:, j : j + 1] == block
        top = jnp.maximum(top, jnp.max(jnp.where(hit, asker_z, -1.0), axis=0, keepdims=True))
        low = jnp.minimum(low, jnp.min(jnp.where(hit, asker_z, 8.0), axis=0, keepdims=True))
    before_lane = (iota((LOCAL, LOCAL), 0) < iota((LOCAL, LOCAL), 1)).astype(BF16)
    before_row = (iota((SLOTS, SLOTS), 1) < iota((SLOTS, SLOTS), 0)).astype(BF16)
    lane = iota((1, LOCAL), 1)
    fits = jnp.ones((1, 1), F32)
    injected, arrived = [], []
    for up in (True, False):
        end = jnp.full((SLOTS, 1), -1.0, F32)
        held = jnp.full((SLOTS, 1), -1.0, F32)
        mine_in = jnp.full((SLOTS, 1), -1.0, F32)
        mine_arrived = jnp.full((SLOTS, 1), -1.0, F32)
        for step in range(PLANES - 1):
            z = step if up else PLANES - 1 - step
            reach = top[:, z * LOCAL : (z + 1) * LOCAL]
            if not up:
                reach = (PLANES - 1) - low[:, z * LOCAL : (z + 1) * LOCAL]
            fresh = (reach > step).astype(F32)
            fresh_rank = jnp.dot(
                jnp.broadcast_to(fresh, (8, LOCAL)).astype(BF16), before_lane, preferred_element_type=F32
            )[0:1]
            free = (end <= step).astype(F32)
            free_rank = jnp.dot(
                before_row, jnp.broadcast_to(free, (SLOTS, HD)).astype(BF16), preferred_element_type=F32
            )[:, 0:1]
            pair = (free_rank == fresh_rank) & (free > 0.5) & (fresh > 0.5)
            code = jnp.sum(jnp.where(pair, 1.0 + lane + LOCAL * reach, 0.0), axis=1, keepdims=True)
            taken = code > 0.5
            new_end = jnp.floor((code - 1.0) / LOCAL)
            new_block = code - 1.0 - LOCAL * new_end
            inject = jnp.where(taken, new_block, -1.0)
            held = jnp.where(taken, z * LOCAL + new_block, jnp.where(free > 0.5, -1.0, held))
            end = jnp.where(taken, new_end, end)
            load = jnp.sum((end > step).astype(F32), axis=0, keepdims=True)
            fits = fits * (load <= SHORT_CAPS[min(step, 3)]).astype(F32)
            mine_in = jnp.where(my_z == z, inject, mine_in)
            mine_arrived = jnp.where(my_z == (z + 1 if up else z - 1), held, mine_arrived)
        injected.append(mine_in)
        arrived.append(mine_arrived)
    diagonal = iota((SLOTS, SLOTS), 0) == iota((SLOTS, SLOTS), 1)

    def as_row(column):
        return jnp.sum(jnp.where(diagonal, column, 0.0), axis=0, keepdims=True)

    in_up, in_down = as_row(injected[0]), as_row(injected[1])
    at_up, at_down = as_row(arrived[0]), as_row(arrived[1])
    rows = iota((8, HD), 0)
    out = jnp.where(rows == 0, in_up[:, :HD], 0.0)
    out = jnp.where(rows == 1, in_up[:, HD:], out)
    out = jnp.where(rows == 2, in_down[:, :HD], out)
    out = jnp.where(rows == 3, in_down[:, HD:], out)
    out = jnp.where(rows == 4, fits, out)
    table_ref[1] = out.astype(jnp.int32)

    slot = iota((1, SLOTS), 1)
    mine = jnp.zeros((PLANE, HD), F32)
    for z in range(PLANES):
        mine = jnp.where(my_z == z, lists[z * PLANE : (z + 1) * PLANE], mine)
    place = jnp.zeros((PLANE, HD), F32)
    lanes = iota((PLANE, HD), 1)
    z_here = my_z.astype(F32)
    for j in range(REQ):
        wanted = mine[:, j : j + 1]
        owner_z = jnp.floor(wanted / LOCAL)
        slot_up = jnp.sum(jnp.where(at_up == wanted, slot, 0.0), axis=1, keepdims=True)
        slot_down = jnp.sum(jnp.where(at_down == wanted, slot, 0.0), axis=1, keepdims=True)
        found = jnp.where(owner_z == z_here, wanted - LOCAL * owner_z, LOCAL + SLOTS + slot_down)
        found = jnp.where(owner_z < z_here, LOCAL + slot_up, found)
        place = jnp.where(lanes == j, found, place)
    table_ref[0] = place.astype(jnp.int32)


def spread_kernel(
    ids_ref, mk_ref, mv_ref, *rest
):
    pools = rest[:CHUNKS]
    table_ref, line, lists, send1, recv1, send2, recv2, send_a, recv_a, own_sem = rest[CHUNKS:]
    me = lax.axis_index("ctx")
    z, p = me // PLANE, me % PLANE
    x, core = p // 2, p % 2

    def in_plane(r):
        return {"ctx": z * PLANE + (p + r) % PLANE}

    def on_line(r):
        return {"ctx": ((z + r) % PLANES) * PLANE + p}

    greet([(in_plane(r), None) for r in range(1, 8)] + [(on_line(r), None) for r in range(1, 8)])

    lanes = lax.broadcasted_iota(jnp.int32, (8, HD), 1)
    row = jnp.zeros((8, HD), jnp.int32)
    for j in range(REQ):
        row = jnp.where(lanes == j, ids_ref[j // 4, j % 4], row)
    line[p] = row

    def copy1(r):
        return pltpu.make_async_remote_copy(
            src_ref=line.at[p],
            dst_ref=line.at[p],
            send_sem=send1.at[r],
            recv_sem=recv1.at[p],
            device_id=in_plane(r),
            device_id_type=MESH,
        )

    def arrival1(r):
        q = (p + r) % PLANE
        return pltpu.make_async_remote_copy(
            src_ref=line.at[q],
            dst_ref=line.at[q],
            send_sem=send1.at[r],
            recv_sem=recv1.at[q],
            device_id=in_plane(r),
            device_id_type=MESH,
        )

    for r in range(1, 8):
        copy1(r).start()

    def part(r, chunk, ref):
        q = (p + r) % PLANE
        return ref.at[:, pl.ds(chunk * ROWS, ROWS), pl.ds(pl.multiple_of((q // 2) * HD, HD), HD)]

    def copy_a(r, chunk, ref):
        return pltpu.make_async_remote_copy(
            src_ref=part(r, chunk, ref),
            dst_ref=pools[chunk].at[pl.ds(p * 8, 8)],
            send_sem=send_a.at[chunk, r],
            recv_sem=recv_a.at[chunk, p],
            device_id=in_plane(r),
            device_id_type=MESH,
        )

    def arrival_a(r, chunk):
        q = (p + r) % PLANE
        return pltpu.make_async_remote_copy(
            src_ref=part(r, chunk, mk_ref),
            dst_ref=pools[chunk].at[pl.ds(q * 8, 8)],
            send_sem=send_a.at[chunk, r],
            recv_sem=recv_a.at[chunk, q],
            device_id=in_plane(r),
            device_id_type=MESH,
        )

    for chunk in range(CHUNKS):
        for r in (4, 3, 5, 2, 6, 1, 7):
            to_core = (core + r) % 2

            @pl.when(to_core == 0)
            def _():
                copy_a(r, chunk, mk_ref).start()

            @pl.when(to_core == 1)
            def _():
                copy_a(r, chunk, mv_ref).start()

        def own(ref, chunk=chunk):
            return pltpu.make_async_copy(
                part(0, chunk, ref), pools[chunk].at[pl.ds(p * 8, 8)], own_sem.at[chunk]
            )

        @pl.when(core == 0)
        def _():
            own(mk_ref).start()

        @pl.when(core == 1)
        def _():
            own(mv_ref).start()

    for r in range(1, 8):
        arrival1(r).wait_recv()
    rows = lax.broadcasted_iota(jnp.int32, (8, HD), 0)
    whole = jnp.zeros((8, HD), jnp.int32)
    for q in range(PLANE):
        whole = jnp.where(rows == q, line[q], whole)
    lists[z] = whole

    def copy2(r):
        return pltpu.make_async_remote_copy(
            src_ref=lists.at[z],
            dst_ref=lists.at[z],
            send_sem=send2.at[r],
            recv_sem=recv2.at[z],
            device_id=on_line(r),
            device_id_type=MESH,
        )

    def arrival2(r):
        q = (z + r) % PLANES
        return pltpu.make_async_remote_copy(
            src_ref=lists.at[q],
            dst_ref=lists.at[q],
            send_sem=send2.at[r],
            recv_sem=recv2.at[q],
            device_id=on_line(r),
            device_id_type=MESH,
        )

    for r in range(1, 8):
        copy2(r).start()
    for r in range(1, 8):
        arrival2(r).wait_recv()
    schedule(lists[...].reshape(PLANES * PLANE, HD).astype(F32), z, table_ref)

    for r in range(1, 8):
        copy1(r).wait_send()
        copy2(r).wait_send()
    for chunk in range(CHUNKS):
        pltpu.make_async_copy(
            part(0, chunk, mk_ref), pools[chunk].at[pl.ds(p * 8, 8)], own_sem.at[chunk]
        ).wait()
        for r in range(1, 8):
            copy_a(r, chunk, mk_ref).wait_send()
            arrival_a(r, chunk).wait_recv()


def spread(retrieval, mk, mv):
    return pl.pallas_call(
        spread_kernel,
        out_shape=[jax.ShapeDtypeStruct((LOCAL, ROWS, HD), BF16)] * CHUNKS
        + [jax.ShapeDtypeStruct((2, 8, HD), jnp.int32)],
        in_specs=[SMEM, ANY, ANY],
        out_specs=[ANY] * CHUNKS + [VMEM],
        scratch_shapes=[
            pltpu.VMEM((PLANE, 8, HD), jnp.int32),
            pltpu.VMEM((PLANES, 8, HD), jnp.int32),
            pltpu.SemaphoreType.DMA((8,)),
            pltpu.SemaphoreType.DMA((8,)),
            pltpu.SemaphoreType.DMA((8,)),
            pltpu.SemaphoreType.DMA((8,)),
            pltpu.SemaphoreType.DMA((CHUNKS, 8)),
            pltpu.SemaphoreType.DMA((CHUNKS, 8)),
            pltpu.SemaphoreType.DMA((CHUNKS,)),
        ],
        compiler_params=pltpu.CompilerParams(
            collective_id=0, has_side_effects=True, vmem_limit_bytes=32 << 20
        ),
        name="spread_blocks",
    )(retrieval, mk, mv)


def attend_kernel(caps, group, delay, *refs):
    slots = caps[-1]
    groups = slots // group
    table, gate_ref, q_ref, k_ref, v_ref, gain_ref = refs[:6]
    rest = list(refs[6:])

    def take(n):
        got = rest[:n]
        del rest[:n]
        return got

    given = take(CHUNKS)
    (out_ref,) = take(1)
    near_k, near_v, mixed = take(3)
    pools, ups, downs = take(CHUNKS), take(CHUNKS), take(CHUNKS)
    ups_out, downs_out = take(CHUNKS), take(CHUNKS)
    parts_out, parts = take(CHUNKS), take(CHUNKS)
    squares_out, squares = take(2)
    (
        pool_sem,
        own_sem,
        halo_send,
        halo_recv,
        up_send,
        up_recv,
        down_send,
        down_recv,
        part_send,
        part_recv,
        sq_send,
        sq_recv,
    ) = rest

    me = lax.axis_index("ctx")
    mem = lax.axis_index("mem")
    z, p = me // PLANE, me % PLANE
    last = PLANES * PLANE - 1

    def in_plane(r):
        return {"ctx": z * PLANE + (p + r) % PLANE}

    def mem_peer(r):
        return {"mem": (mem + r) % 8}

    above, below = {"ctx": me + PLANE}, {"ctx": me - PLANE}
    loads = [
        pltpu.make_async_copy(given[c], pools[c], pool_sem.at[c]) for c in range(CHUNKS)
    ] + [
        pltpu.make_async_copy(k_ref, near_k.at[pl.ds(2 * TOK, TOK)], own_sem.at[0]),
        pltpu.make_async_copy(v_ref, near_v.at[pl.ds(2 * TOK, TOK)], own_sem.at[1]),
    ]
    for load in loads:
        load.start()

    greet(
        [(in_plane(r), None) for r in range(1, 8)]
        + [(mem_peer(r), None) for r in range(1, 8)]
        + [(above, z < PLANES - 1), (below, z > 0)]
        + [({"ctx": me + d}, me + d <= last) for d in (1, 2)]
        + [({"ctx": me - d}, me - d >= 0) for d in (1, 2)]
    )

    def halo(d, which):
        ref, near = ((k_ref, near_k), (v_ref, near_v))[which]
        return pltpu.make_async_remote_copy(
            src_ref=ref,
            dst_ref=near.at[pl.ds((2 - d) * TOK, TOK)],
            send_sem=halo_send.at[2 * d - 2 + which],
            recv_sem=halo_recv.at[2 * d - 2 + which],
            device_id={"ctx": me + d},
            device_id_type=MESH,
        )

    for d in (1, 2):

        @pl.when(me + d <= last)
        def _():
            halo(d, 0).start()
            halo(d, 1).start()

        @pl.when(me - d < 0)
        def _():
            near_k[pl.ds((2 - d) * TOK, TOK)] = jnp.zeros((TOK, HEADS_HERE * HD), BF16)
            near_v[pl.ds((2 - d) * TOK, TOK)] = jnp.zeros((TOK, HEADS_HERE * HD), BF16)

    for load in loads:
        load.wait()

    caps_g = [c // group for c in caps]

    def cap_at(step):
        value = jnp.int32(caps_g[3])
        for i in (2, 1, 0):
            value = jnp.where(step == i, caps_g[i], value)
        return value

    def conveyor(k, step, target, pool, into, onward, send, recv, row):
        cap = cap_at(step)
        position = jnp.where(step <= 3, k + groups - cap, k - delay * (step - 3))
        inside = (position >= 0) & (position < CHUNKS * groups)
        at = jnp.maximum(position, 0)
        chunk = at // groups
        g = groups - 1 - at % groups
        active = inside & (g < cap)
        incoming = (step > 0) & (g < cap_at(step - 1))

        def copy(c):
            span = pl.ds(g * group, group)
            return pltpu.make_async_remote_copy(
                src_ref=onward[c].at[span],
                dst_ref=into[c].at[span],
                send_sem=send.at[c, g],
                recv_sem=recv.at[c, g],
                device_id=target,
                device_id_type=MESH,
            )

        for c in range(CHUNKS):

            @pl.when(active & (chunk == c))
            def _(c=c):
                @pl.when(incoming)
                def _():
                    copy(c).wait_recv()

                @pl.when(step < PLANES - 1)
                def _():
                    for i in range(group):
                        slot = g * group + i
                        inject = table[1, row + slot // HD, slot % HD]
                        local = pool[c][jnp.maximum(inject, 0)]
                        onward[c][slot] = jnp.where(inject >= 0, local, into[c][slot])
                    copy(c).start()

    def part_copy(c, r):
        q = (p + r) % PLANE
        return pltpu.make_async_remote_copy(
            src_ref=parts_out[c].at[q],
            dst_ref=parts[c].at[p],
            send_sem=part_send.at[c, r],
            recv_sem=part_recv.at[c, p],
            device_id=in_plane(r),
            device_id_type=MESH,
        )

    def part_arrival(c, r):
        q = (p + r) % PLANE
        return pltpu.make_async_remote_copy(
            src_ref=parts_out[c].at[q],
            dst_ref=parts[c].at[q],
            send_sem=part_send.at[c, r],
            recv_sem=part_recv.at[c, q],
            device_id=in_plane(r),
            device_id_type=MESH,
        )

    def hand_out(c):
        def pick(q, j):
            place = table[0, q, j]
            own = pools[c][jnp.minimum(place, LOCAL - 1)]
            from_below = ups[c][jnp.clip(place - LOCAL, 0, slots - 1)]
            from_above = downs[c][jnp.clip(place - LOCAL - SLOTS, 0, slots - 1)]
            return jnp.where(
                place < LOCAL, own, jnp.where(place < LOCAL + SLOTS, from_below, from_above)
            )

        for r in (4, 3, 5, 2, 6, 1, 7):
            q = (p + r) % PLANE
            for j in range(REQ):
                parts_out[c][q, j] = pick(q, j)
            part_copy(c, r).start()
        for j in range(REQ):
            parts[c][p, j] = pick(p, j)

    def window_piece(head, tile):
        columns = pl.ds(pl.multiple_of(head * HD, HD), HD)
        rows = pl.ds(pl.multiple_of(tile * 128, 128), 128)
        near = pl.ds(pl.multiple_of(tile * 128, 128), 640)
        scores = lax.dot_general(
            q_ref[rows, columns],
            near_k[near, columns],
            (((1,), (1,)), ((), ())),
            preferred_element_type=F32,
        )
        key = lax.broadcasted_iota(jnp.int32, (128, 640), 1)
        ahead = key - lax.broadcasted_iota(jnp.int32, (128, 640), 0)
        first = me * TOK - 2 * TOK + tile * 128
        allowed = (ahead > 0) & (ahead <= 512) & (key >= -first)
        scores = jnp.where(allowed, scores * SCALE, -jnp.inf)
        weights = jnp.exp(scores - jnp.max(scores, axis=1, keepdims=True))
        total = jnp.sum(weights, axis=1, keepdims=True)
        product = jnp.dot(weights.astype(BF16), near_v[near, columns], preferred_element_type=F32)
        mixed[rows, columns] = product / total

    steps = CHUNKS * groups + 4 * delay
    far = jnp.maximum(z, PLANES - 1 - z) - 3
    pieces = 2 * HEADS_HERE
    every = max(1, (steps - 12) // (pieces + 2))
    first_piece = steps - 4 - every * pieces

    def step_body(k, carry):
        conveyor(k, z, above, pools, ups, ups_out, up_send, up_recv, 0)
        conveyor(k, PLANES - 1 - z, below, pools, downs, downs_out, down_send, down_recv, 2)
        for c in range(CHUNKS):

            @pl.when(k == (c + 1) * groups - 1 + delay * far)
            def _(c=c):
                hand_out(c)

        @pl.when(k == first_piece)
        def _():
            for d in (1, 2):

                @pl.when(me - d >= 0)
                def _():
                    halo(d, 0).wait_recv()
                    halo(d, 1).wait_recv()

        since = k - first_piece
        piece = jnp.maximum(since, 0) // every

        @pl.when((since >= 0) & (since % every == 0) & (piece < pieces))
        def _():
            window_piece(piece // 2, piece % 2)

        return carry

    lax.fori_loop(0, steps, step_body, 0)

    for c in range(CHUNKS):
        for r in range(1, 8):
            part_arrival(c, r).wait_recv()

    opened = 1.0 / (1.0 + jnp.exp(-gate_ref[...]))
    eye = lax.broadcasted_iota(jnp.int32, (128, 128), 0) == lax.broadcasted_iota(
        jnp.int32, (128, 128), 1
    )
    for tile in range(2):
        rows = pl.ds(tile * 128, 128)
        total_square = jnp.zeros((128, 1), F32)
        for head in range(HEADS_HERE):
            columns = pl.ds(head * HD, HD)
            keys = [parts[c][2 * head, 4 * tile : 4 * tile + 4].reshape(4 * ROWS, HD) for c in range(CHUNKS)]
            vals = [parts[c][2 * head + 1, 4 * tile : 4 * tile + 4].reshape(4 * ROWS, HD) for c in range(CHUNKS)]
            scores = lax.dot_general(
                q_ref[rows, columns],
                jnp.concatenate(keys, axis=0),
                (((1,), (1,)), ((), ())),
                preferred_element_type=F32,
            ) * SCALE
            weights = jnp.exp(scores - jnp.max(scores, axis=1, keepdims=True))
            total = jnp.sum(weights, axis=1, keepdims=True)
            product = jnp.dot(
                weights.astype(BF16), jnp.concatenate(vals, axis=0), preferred_element_type=F32
            )
            share = opened[:, head : head + 1]
            both = share * (product / total) + (1.0 - share) * mixed[rows, columns]
            mixed[rows, columns] = both
            total_square += jnp.sum(both * both, axis=1, keepdims=True)
        squares_out[pl.ds(tile * 8, 8)] = jnp.broadcast_to(
            jnp.sum(jnp.where(eye, total_square, 0.0), axis=0, keepdims=True), (8, 128)
        )

    def square_copy(r):
        return pltpu.make_async_remote_copy(
            src_ref=squares_out,
            dst_ref=squares.at[mem],
            send_sem=sq_send.at[r],
            recv_sem=sq_recv.at[mem],
            device_id=mem_peer(r),
            device_id_type=MESH,
        )

    def square_arrival(r):
        return pltpu.make_async_remote_copy(
            src_ref=squares_out,
            dst_ref=squares.at[(mem + r) % 8],
            send_sem=sq_send.at[r],
            recv_sem=sq_recv.at[(mem + r) % 8],
            device_id=mem_peer(r),
            device_id_type=MESH,
        )

    for r in (4, 1, 2, 3, 5, 6, 7):
        square_copy(r).start()
    squares[mem] = squares_out[...]
    for r in range(1, 8):
        square_arrival(r).wait_recv()
    summed = squares[0]
    for m in range(1, 8):
        summed = summed + squares[m]
    for tile in range(2):
        rows = pl.ds(tile * 128, 128)
        column = jnp.sum(
            jnp.where(eye, summed[tile * 8 : tile * 8 + 1], 0.0), axis=1, keepdims=True
        )
        factor = lax.rsqrt(column / FEATURES + 1e-6)
        out_ref[rows] = (mixed[rows] * gain_ref[...] * factor).astype(BF16)

    for r in range(1, 8):
        square_copy(r).wait_send()
        for c in range(CHUNKS):
            part_copy(c, r).wait_send()
    for d in (1, 2):

        @pl.when(me + d <= last)
        def _():
            halo(d, 0).wait_send()
            halo(d, 1).wait_send()

    for step, into, onward, send, recv, target in (
        (z, ups, ups_out, up_send, up_recv, above),
        (PLANES - 1 - z, downs, downs_out, down_send, down_recv, below),
    ):

        @pl.when(step < PLANES - 1)
        def _():
            def sent(g, carry):
                span = pl.ds(g * group, group)
                for c in range(CHUNKS):
                    pltpu.make_async_remote_copy(
                        src_ref=onward[c].at[span],
                        dst_ref=into[c].at[span],
                        send_sem=send.at[c, g],
                        recv_sem=recv.at[c, g],
                        device_id=target,
                        device_id_type=MESH,
                    ).wait_send()
                return carry

            lax.fori_loop(0, cap_at(step), sent, 0)


def attend(caps, group, delay, collective_id, table, gate, q, k, v, gain, *pools):
    slots = caps[-1]
    groups = slots // group
    ring = [pltpu.VMEM((slots, ROWS, HD), BF16)] * CHUNKS
    hand = [pltpu.VMEM((PLANE, REQ, ROWS, HD), BF16)] * CHUNKS
    dma = pltpu.SemaphoreType.DMA
    return pl.pallas_call(
        functools.partial(attend_kernel, caps, group, delay),
        out_shape=jax.ShapeDtypeStruct((TOK, HEADS_HERE * HD), BF16),
        in_specs=[SMEM, VMEM, VMEM, ANY, ANY, VMEM] + [ANY] * CHUNKS,
        out_specs=VMEM,
        scratch_shapes=[
            pltpu.VMEM((3 * TOK, HEADS_HERE * HD), BF16),
            pltpu.VMEM((3 * TOK, HEADS_HERE * HD), BF16),
            pltpu.VMEM((TOK, HEADS_HERE * HD), F32),
            *[pltpu.VMEM((LOCAL, ROWS, HD), BF16)] * CHUNKS,
            *ring,
            *ring,
            *ring,
            *ring,
            *hand,
            *hand,
            pltpu.VMEM((16, HD), F32),
            pltpu.VMEM((8, 16, HD), F32),
            dma((CHUNKS,)),
            dma((2,)),
            dma((4,)),
            dma((4,)),
            dma((CHUNKS, groups)),
            dma((CHUNKS, groups)),
            dma((CHUNKS, groups)),
            dma((CHUNKS, groups)),
            dma((CHUNKS, 8)),
            dma((CHUNKS, 8)),
            dma((8,)),
            dma((8,)),
        ],
        compiler_params=pltpu.CompilerParams(
            collective_id=collective_id, has_side_effects=True, vmem_limit_bytes=48 << 20
        ),
        name="attend_" + str(slots),
    )(table, gate, q, k, v, gain, *pools)


def shards(queries, keys, values, memory_keys, memory_values, retrieval, gate, gain):
    *pools, table = spread(retrieval, memory_keys, memory_values)
    fits = table[1, 4, 0] > 0
    operands = (
        table,
        gate.reshape(1, -1),
        queries,
        keys,
        values,
        gain.reshape(1, -1),
        *pools,
    )
    return lax.cond(
        fits,
        functools.partial(attend, SHORT_CAPS, 8, 2, 1),
        functools.partial(attend, LONG_CAPS, 16, 2, 2),
        *operands,
    )


def solution(mesh):
    in_specs = (
        P("ctx", "mem"),
        P("ctx", "mem"),
        P("ctx", "mem"),
        P("ctx", None, "mem"),
        P("ctx", None, "mem"),
        P("ctx", None),
        P("mem"),
        P("mem"),
    )
    return jax.shard_map(
        shards, mesh=mesh, in_specs=in_specs, out_specs=P("ctx", "mem"), check_vma=False
    )
```

time: 496 us -> 147 us (0.30)
  the two profiles are of different devices: /device:TPU:128 before, /device:TPU:1 now
where the time goes in v1:
time: 147 us; the launch traced here: 146 us
  Pallas kernels  141 us (96%)
  local copies, waits for them, and re-layouts  4.63 us (3%)
    pallas_call x1, Pallas kernels, attend(): pl.pallas_call(functools.partial(attend_kernel, caps, group, delay), out_...  112 us
    pallas_call x1, Pallas kernels, spread(): pl.pallas_call(spread_kernel, out_shape=[jax.ShapeDtypeStruct((LOCAL, ROW...  28.6 us
    unnamed x17, local copies, waits for them, and re-layouts  4.12 us

profile of v1, /device:TPU:1, one launch (start us, length us, event | category | flops | bytes accessed | tf_op | source)
XLA Modules:
  0.0 146.1 jit_solution(11289666674737563629)
XLA Ops:
  0.0 0.0 copy-start.2
  0.0 0.7 copy-done.2
  0.7 0.0 copy-start
  0.7 1.0 copy-done
  1.7 0.0 copy-start.1
  1.7 1.0 copy-done.1
  2.8 0.0 copy-start.3
  2.8 0.0 copy-start.4
  2.8 0.0 copy-start.5
  2.8 28.6 %spread_blocks.1 = (bf16[64,32,128]{2,1,0:T(8,128)(2,1)S(1)}, bf16[64,32,128]{2,1,0:T(8,128)(2,1)S(1)}, s32[2,8,128]{2,1,0:T(8,128)S(1)}) custom-call(s32[2,4]{1,0:T(2,128)S(1)} %copy-done.2, bf16[8,64,512]{2,1,0:T(8,128)(2,1)S(1)} %copy-done, bf16[8,64,512]{2,1,0:T(8,128)(2,1)S(1)} %copy-done.1), custom_call_target="tpu_custom_call" | custom-call | tf_op jit(solution)/shard_map/spread_blocks/pallas_call | solution.py:281
  31.4 0.5 slice.3
  32.6 0.0 copy-start.6
  32.6 0.0 copy-start.7
  32.6 0.0 copy-done.3
  32.6 0.0 copy-done.4
  32.6 0.0 copy-done.5
  32.6 0.6 copy-done.6
  33.3 0.0 copy-done.7
  33.3 112.1 %conditional.1 = (bf16[256,512]{1,0:T(8,128)(2,1)S(1)}) conditional(s32[]{:T(128)} %bitcast, (s32[2,8,128]{2,1,0:T(8,128)S(1)}, f32[1,4]{1,0:T(1,128)S(1)}, bf16[256,512]{1,0:T(8,128)(2,1)S(1)}, bf16[256,512]{1,0:T(8,128)(2,1)S(1)}, bf16[256,512]{1,0:T(8,128)(2,1)S(1)}, /*index=5*/f32[1,512]{1,0:T(1,128)S(1)}, bf16[64,32,128]{2,1,0:T(8,128)(2,1)S(1)}, ...), branch_computations={%region_0.0_spmd, %region_1.0_spmd} | conditional | bytes 8 | solution.py:694
  33.3 112.1 %attend_120.1 = bf16[256,512]{1,0:T(8,128)(2,1)S(1)} custom-call(s32[2,8,128]{2,1,0:T(8,128)S(1)} %get-tuple-element.48.refs_0_, f32[1,4]{1,0:T(1,128)S(1)} %get-tuple-element.49.refs_1_, bf16[256,512]{1,0:T(8,128)(2,1)S(1)} %get-tuple-element.50.refs_2_, bf16[256,512]{1,0:T(8,128)(2,1)S(1)} %get-tuple-element.51.refs_3_, ...), custom_call_target="tpu_custom_call" | custom-call | tf_op jit(solution)/shard_map/cond/branch_1_fun/attend_120/pallas_call | solution.py:644
  145.4 0.7 copy.14
Async XLA Ops:
  0.0 0.7 copy-start.2
  0.7 1.0 copy-start
  1.7 1.0 copy-start.1
  2.8 29.8 %copy-start.3 = (bf16[256,512]{1,0:T(8,128)(2,1)S(1)}, bf16[256,512]{1,0:T(8,128)(2,1)}, u32[]{:S(2)}) copy-start(bf16[256,512]{1,0:T(8,128)(2,1)} %param.10) | copy-start | bytes 786436
  2.8 29.8 %copy-start.4 = (bf16[256,512]{1,0:T(8,128)(2,1)S(1)}, bf16[256,512]{1,0:T(8,128)(2,1)}, u32[]{:S(2)}) copy-start(bf16[256,512]{1,0:T(8,128)(2,1)} %param.11) | copy-start | bytes 786436
  2.8 29.9 %copy-start.5 = (bf16[256,512]{1,0:T(8,128)(2,1)S(1)}, bf16[256,512]{1,0:T(8,128)(2,1)}, u32[]{:S(2)}) copy-start(bf16[256,512]{1,0:T(8,128)(2,1)} %param.12) | copy-start | bytes 786436
  32.6 0.7 copy-start.6
  32.6 0.7 copy-start.7

commit v2 on v1

--- a/solution.py
+++ b/solution.py
@@ -9,7 +9,7 @@
 from jax.sharding import PartitionSpec as P
 
 MESH = pl.DeviceIdType.MESH
-ANY = pl.BlockSpec(memory_space=pl.ANY)
+HBM = pl.BlockSpec(memory_space=pltpu.HBM)
 VMEM = pl.BlockSpec(memory_space=pltpu.VMEM)
 SMEM = pl.BlockSpec(memory_space=pltpu.SMEM)
 F32 = jnp.float32
@@ -29,8 +29,12 @@
 ROWS = BLK // CHUNKS
 SCALE = 1.0 / math.sqrt(HD)
 
-SHORT_CAPS = (56, 88, 112, 120)
-LONG_CAPS = (64, 128, 192, 256)
+TIERS = (
+    ((48, 80, 96, 104), 8, (3, 7, 10, 11), 16),
+    ((56, 88, 104, 112), 8, (3, 7, 10, 11), 16),
+    ((64, 128, 192, 256), 16, (2, 4, 6, 8), 0),
+)
+REACHES = (7, 1, 2, 3, 4, 5, 6)
 
 
 def iota(shape, dim):
@@ -64,11 +68,17 @@
         top = jnp.maximum(top, jnp.max(jnp.where(hit, asker_z, -1.0), axis=0, keepdims=True))
         low = jnp.minimum(low, jnp.min(jnp.where(hit, asker_z, 8.0), axis=0, keepdims=True))
     before_lane = (iota((LOCAL, LOCAL), 0) < iota((LOCAL, LOCAL), 1)).astype(BF16)
-    before_row = (iota((SLOTS, SLOTS), 1) < iota((SLOTS, SLOTS), 0)).astype(BF16)
+    after_row = (iota((SLOTS, SLOTS), 1) > iota((SLOTS, SLOTS), 0)).astype(BF16)
+    before_kind = (iota((8, 8), 1) < iota((8, 8), 0)).astype(BF16)
+    slot_column = iota((SLOTS, 1), 0)
+    kind = jnp.full((8, 1), -1.0, F32)
+    for i, reach in enumerate(REACHES):
+        kind = jnp.where(iota((8, 1), 0) == i, reach, kind)
     lane = iota((1, LOCAL), 1)
-    fits = jnp.ones((1, 1), F32)
+    fits = [jnp.ones((1, 1), F32) for _ in TIERS[:-1]]
     injected, arrived = [], []
     for up in (True, False):
+        height = jnp.zeros((1, 1), F32)
         end = jnp.full((SLOTS, 1), -1.0, F32)
         held = jnp.full((SLOTS, 1), -1.0, F32)
         mine_in = jnp.full((SLOTS, 1), -1.0, F32)
@@ -79,12 +89,21 @@
             if not up:
                 reach = (PLANES - 1) - low[:, z * LOCAL : (z + 1) * LOCAL]
             fresh = (reach > step).astype(F32)
-            fresh_rank = jnp.dot(
-                jnp.broadcast_to(fresh, (8, LOCAL)).astype(BF16), before_lane, preferred_element_type=F32
-            )[0:1]
-            free = (end <= step).astype(F32)
+            kinds = (reach == kind).astype(F32) * fresh
+            of_kind = jnp.dot(kinds.astype(BF16), before_lane, preferred_element_type=F32)
+            earlier = jnp.dot(
+                before_kind,
+                jnp.broadcast_to(jnp.sum(kinds, axis=1, keepdims=True), (8, HD)).astype(BF16),
+                preferred_element_type=F32,
+            )[:, 0:1]
+            fresh_rank = jnp.sum(kinds * (of_kind + earlier), axis=0, keepdims=True)
+            load = jnp.sum((end > step).astype(F32), axis=0, keepdims=True) + jnp.sum(
+                fresh, axis=1, keepdims=True
+            )
+            height = jnp.maximum(height, load)
+            free = ((end <= step) & (slot_column < height)).astype(F32)
             free_rank = jnp.dot(
-                before_row, jnp.broadcast_to(free, (SLOTS, HD)).astype(BF16), preferred_element_type=F32
+                after_row, jnp.broadcast_to(free, (SLOTS, HD)).astype(BF16), preferred_element_type=F32
             )[:, 0:1]
             pair = (free_rank == fresh_rank) & (free > 0.5) & (fresh > 0.5)
             code = jnp.sum(jnp.where(pair, 1.0 + lane + LOCAL * reach, 0.0), axis=1, keepdims=True)
@@ -92,10 +111,19 @@
             new_end = jnp.floor((code - 1.0) / LOCAL)
             new_block = code - 1.0 - LOCAL * new_end
             inject = jnp.where(taken, new_block, -1.0)
-            held = jnp.where(taken, z * LOCAL + new_block, jnp.where(free > 0.5, -1.0, held))
+            held = jnp.where(taken, z * LOCAL + new_block, jnp.where(end <= step, -1.0, held))
             end = jnp.where(taken, new_end, end)
-            load = jnp.sum((end > step).astype(F32), axis=0, keepdims=True)
-            fits = fits * (load <= SHORT_CAPS[min(step, 3)]).astype(F32)
+            fits = [
+                fit * (load <= tier[0][min(step, 3)]).astype(F32)
+                for fit, tier in zip(fits, TIERS)
+            ]
+            if step == PLANES - 2:
+                lowest = jnp.min(
+                    jnp.where(end > step, slot_column, SLOTS), axis=0, keepdims=True
+                )
+                fits = [
+                    fit * (lowest >= tier[3]).astype(F32) for fit, tier in zip(fits, TIERS)
+                ]
             mine_in = jnp.where(my_z == z, inject, mine_in)
             mine_arrived = jnp.where(my_z == (z + 1 if up else z - 1), held, mine_arrived)
         injected.append(mine_in)
@@ -112,7 +140,7 @@
     out = jnp.where(rows == 1, in_up[:, HD:], out)
     out = jnp.where(rows == 2, in_down[:, :HD], out)
     out = jnp.where(rows == 3, in_down[:, HD:], out)
-    out = jnp.where(rows == 4, fits, out)
+    out = jnp.where(rows == 4, len(fits) - sum(fits), out)
     table_ref[1] = out.astype(jnp.int32)
 
     slot = iota((1, SLOTS), 1)
@@ -134,10 +162,24 @@
 
 
 def spread_kernel(
-    ids_ref, mk_ref, mv_ref, *rest
+    ids_ref, mk_ref, mv_ref, k_ref, v_ref, *rest
 ):
     pools = rest[:CHUNKS]
-    table_ref, line, lists, send1, recv1, send2, recv2, send_a, recv_a, own_sem = rest[CHUNKS:]
+    (
+        edge_ref,
+        table_ref,
+        line,
+        lists,
+        send1,
+        recv1,
+        send2,
+        recv2,
+        send_a,
+        recv_a,
+        own_sem,
+        edge_send,
+        edge_recv,
+    ) = rest[CHUNKS:]
     me = lax.axis_index("ctx")
     z, p = me // PLANE, me % PLANE
     x, core = p // 2, p % 2
@@ -229,6 +271,46 @@
         @pl.when(core == 1)
         def _():
             own(mv_ref).start()
+
+    def edge_part(q):
+        ref = v_ref if q % 2 else k_ref
+        return ref.at[:, pl.ds(q // 2 * HD, HD)]
+
+    def edge_copy(q):
+        return pltpu.make_async_remote_copy(
+            src_ref=edge_part(q),
+            dst_ref=edge_ref.at[pl.ds(core * TOK, TOK)],
+            send_sem=edge_send.at[q],
+            recv_sem=edge_recv.at[core],
+            device_id={"ctx": z * PLANE + q},
+            device_id_type=MESH,
+        )
+
+    def edge_arrival(source):
+        return pltpu.make_async_remote_copy(
+            src_ref=edge_part(0),
+            dst_ref=edge_ref.at[pl.ds(source * TOK, TOK)],
+            send_sem=edge_send.at[0],
+            recv_sem=edge_recv.at[source],
+            device_id=in_plane(1),
+            device_id_type=MESH,
+        )
+
+    def edge_own(q):
+        return pltpu.make_async_copy(
+            edge_part(q), edge_ref.at[pl.ds(core * TOK, TOK)], own_sem.at[CHUNKS]
+        )
+
+    sends_edge = (x == 3) & (z < PLANES - 1)
+    for q in range(PLANE):
+
+        @pl.when(sends_edge & (p != q))
+        def _(q=q):
+            edge_copy(q).start()
+
+        @pl.when(sends_edge & (p == q))
+        def _(q=q):
+            edge_own(q).start()
 
     for r in range(1, 8):
         arrival1(r).wait_recv()
@@ -268,6 +350,22 @@
     for r in range(1, 8):
         copy1(r).wait_send()
         copy2(r).wait_send()
+    for q in range(PLANE):
+
+        @pl.when(sends_edge & (p != q))
+        def _(q=q):
+            edge_copy(q).wait_send()
+
+        @pl.when(sends_edge & (p == q))
+        def _(q=q):
+            edge_own(q).wait()
+
+    for source in range(2):
+
+        @pl.when((z < PLANES - 1) & (p != 6 + source))
+        def _(source=source):
+            edge_arrival(source).wait_recv()
+
     for chunk in range(CHUNKS):
         pltpu.make_async_copy(
             part(0, chunk, mk_ref), pools[chunk].at[pl.ds(p * 8, 8)], own_sem.at[chunk]
@@ -277,13 +375,16 @@
             arrival_a(r, chunk).wait_recv()
 
 
-def spread(retrieval, mk, mv):
+def spread(retrieval, mk, mv, k, v):
     return pl.pallas_call(
         spread_kernel,
         out_shape=[jax.ShapeDtypeStruct((LOCAL, ROWS, HD), BF16)] * CHUNKS
-        + [jax.ShapeDtypeStruct((2, 8, HD), jnp.int32)],
-        in_specs=[SMEM, ANY, ANY],
-        out_specs=[ANY] * CHUNKS + [VMEM],
+        + [
+            jax.ShapeDtypeStruct((2 * TOK, HD), BF16),
+            jax.ShapeDtypeStruct((2, 8, HD), jnp.int32),
+        ],
+        in_specs=[SMEM, HBM, HBM, HBM, HBM],
+        out_specs=[pl.BlockSpec(memory_space=pl.ANY)] * (CHUNKS + 1) + [VMEM],
         scratch_shapes=[
             pltpu.VMEM((PLANE, 8, HD), jnp.int32),
             pltpu.VMEM((PLANES, 8, HD), jnp.int32),
@@ -293,19 +394,22 @@
             pltpu.SemaphoreType.DMA((8,)),
             pltpu.SemaphoreType.DMA((CHUNKS, 8)),
             pltpu.SemaphoreType.DMA((CHUNKS, 8)),
-            pltpu.SemaphoreType.DMA((CHUNKS,)),
+            pltpu.SemaphoreType.DMA((CHUNKS + 1,)),
+            pltpu.SemaphoreType.DMA((8,)),
+            pltpu.SemaphoreType.DMA((2,)),
         ],
         compiler_params=pltpu.CompilerParams(
-            collective_id=0, has_side_effects=True, vmem_limit_bytes=32 << 20
+            collective_id=0, has_side_effects=True, vmem_limit_bytes=62 << 20
         ),
         name="spread_blocks",
-    )(retrieval, mk, mv)
-
-
-def attend_kernel(caps, group, delay, *refs):
+    )(retrieval, mk, mv, k, v)
+
+
+def attend_kernel(tier, *refs):
+    caps, group, lags, left_out = tier
     slots = caps[-1]
     groups = slots // group
-    table, gate_ref, q_ref, k_ref, v_ref, gain_ref = refs[:6]
+    table, gate_hbm, q_hbm, k_ref, v_ref, gain_hbm = refs[:6]
     rest = list(refs[6:])
 
     def take(n):
@@ -314,12 +418,13 @@
         return got
 
     given = take(CHUNKS)
+    (edge_ref,) = take(1)
     (out_ref,) = take(1)
-    near_k, near_v, mixed = take(3)
+    gate_ref, q_ref, gain_ref, near_k, near_v, mixed = take(6)
     pools, ups, downs = take(CHUNKS), take(CHUNKS), take(CHUNKS)
     ups_out, downs_out = take(CHUNKS), take(CHUNKS)
     parts_out, parts = take(CHUNKS), take(CHUNKS)
-    squares_out, squares = take(2)
+    squares_out, squares, edge_in = take(3)
     (
         pool_sem,
         own_sem,
@@ -333,12 +438,14 @@
         part_recv,
         sq_send,
         sq_recv,
+        edge_sem,
+        pass_send,
+        pass_recv,
     ) = rest
 
     me = lax.axis_index("ctx")
     mem = lax.axis_index("mem")
     z, p = me // PLANE, me % PLANE
-    last = PLANES * PLANE - 1
 
     def in_plane(r):
         return {"ctx": z * PLANE + (p + r) % PLANE}
@@ -352,6 +459,9 @@
     ] + [
         pltpu.make_async_copy(k_ref, near_k.at[pl.ds(2 * TOK, TOK)], own_sem.at[0]),
         pltpu.make_async_copy(v_ref, near_v.at[pl.ds(2 * TOK, TOK)], own_sem.at[1]),
+        pltpu.make_async_copy(q_hbm, q_ref, own_sem.at[2]),
+        pltpu.make_async_copy(gate_hbm, gate_ref, own_sem.at[3]),
+        pltpu.make_async_copy(gain_hbm, gain_ref, own_sem.at[4]),
     ]
     for load in loads:
         load.start()
@@ -360,9 +470,61 @@
         [(in_plane(r), None) for r in range(1, 8)]
         + [(mem_peer(r), None) for r in range(1, 8)]
         + [(above, z < PLANES - 1), (below, z > 0)]
-        + [({"ctx": me + d}, me + d <= last) for d in (1, 2)]
-        + [({"ctx": me - d}, me - d >= 0) for d in (1, 2)]
     )
+
+    def edge_copy():
+        return pltpu.make_async_remote_copy(
+            src_ref=edge_ref,
+            dst_ref=edge_in,
+            send_sem=edge_sem.at[0],
+            recv_sem=edge_sem.at[1],
+            device_id=above,
+            device_id_type=MESH,
+        )
+
+    @pl.when(z < PLANES - 1)
+    def _():
+        edge_copy().start()
+
+    def passed(source, to):
+        near = near_v if source % 2 else near_k
+        columns = pl.ds(source // 2 * HD, HD)
+        came = edge_in if to == 0 else edge_in.at[pl.ds(TOK, TOK)]
+        return came, near.at[pl.ds(0, 2 * TOK if to == 0 else TOK), columns]
+
+    def pass_copy(source, to):
+        came, near = passed(source, to)
+        return pltpu.make_async_remote_copy(
+            src_ref=came,
+            dst_ref=near,
+            send_sem=pass_send.at[to],
+            recv_sem=pass_recv.at[source],
+            device_id={"ctx": z * PLANE + to},
+            device_id_type=MESH,
+        )
+
+    def pass_own(source):
+        came, near = passed(source, source)
+        return pltpu.make_async_copy(came, near, pass_recv.at[source])
+
+    def each_pass(source, remote, local):
+        for to in range(2):
+            if source == to:
+                local(source)
+            else:
+                remote(source, to)
+
+    def pass_on():
+        edge_copy().wait_recv()
+        for source in range(PLANE):
+
+            @pl.when(p == source)
+            def _(source=source):
+                each_pass(
+                    source,
+                    lambda s, t: pass_copy(s, t).start(),
+                    lambda s: pass_own(s).start(),
+                )
 
     def halo(d, which):
         ref, near = ((k_ref, near_k), (v_ref, near_v))[which]
@@ -377,12 +539,12 @@
 
     for d in (1, 2):
 
-        @pl.when(me + d <= last)
+        @pl.when(p + d < PLANE)
         def _():
             halo(d, 0).start()
             halo(d, 1).start()
 
-        @pl.when(me - d < 0)
+        @pl.when((z == 0) & (p < d))
         def _():
             near_k[pl.ds((2 - d) * TOK, TOK)] = jnp.zeros((TOK, HEADS_HERE * HD), BF16)
             near_v[pl.ds((2 - d) * TOK, TOK)] = jnp.zeros((TOK, HEADS_HERE * HD), BF16)
@@ -398,15 +560,24 @@
             value = jnp.where(step == i, caps_g[i], value)
         return value
 
+    def floor_at(step):
+        return jnp.where(step >= PLANES - 2, left_out // group, 0)
+
+    def lag_at(step):
+        value = jnp.int32(0)
+        for i in range(4):
+            value = jnp.where(step == 4 + i, lags[i], value)
+        return value
+
     def conveyor(k, step, target, pool, into, onward, send, recv, row):
         cap = cap_at(step)
-        position = jnp.where(step <= 3, k + groups - cap, k - delay * (step - 3))
+        position = jnp.where(step <= 3, k + groups - cap, k - lag_at(step))
         inside = (position >= 0) & (position < CHUNKS * groups)
         at = jnp.maximum(position, 0)
         chunk = at // groups
         g = groups - 1 - at % groups
         active = inside & (g < cap)
-        incoming = (step > 0) & (g < cap_at(step - 1))
+        incoming = (step > 0) & (g < cap_at(step - 1)) & (g >= floor_at(step - 1))
 
         def copy(c):
             span = pl.ds(g * group, group)
@@ -427,7 +598,7 @@
                 def _():
                     copy(c).wait_recv()
 
-                @pl.when(step < PLANES - 1)
+                @pl.when((step < PLANES - 1) & (g >= floor_at(step)))
                 def _():
                     for i in range(group):
                         slot = g * group + i
@@ -496,10 +667,12 @@
         product = jnp.dot(weights.astype(BF16), near_v[near, columns], preferred_element_type=F32)
         mixed[rows, columns] = product / total
 
-    steps = CHUNKS * groups + 4 * delay
-    far = jnp.maximum(z, PLANES - 1 - z) - 3
+    steps = CHUNKS * groups + max(lags[2], lags[3] - left_out // group)
+    far = jnp.maximum(z, PLANES - 1 - z)
+    far = lag_at(far) - floor_at(far - 1)
     pieces = 2 * HEADS_HERE
     every = max(1, (steps - 12) // (pieces + 2))
+    pass_step = 5
     first_piece = steps - 4 - every * pieces
 
     def step_body(k, carry):
@@ -507,18 +680,32 @@
         conveyor(k, PLANES - 1 - z, below, pools, downs, downs_out, down_send, down_recv, 2)
         for c in range(CHUNKS):
 
-            @pl.when(k == (c + 1) * groups - 1 + delay * far)
+            @pl.when(k == (c + 1) * groups - 1 + far)
             def _(c=c):
                 hand_out(c)
+
+        @pl.when((k == pass_step) & (z > 0))
+        def _():
+            pass_on()
 
         @pl.when(k == first_piece)
         def _():
             for d in (1, 2):
 
-                @pl.when(me - d >= 0)
+                @pl.when(p >= d)
                 def _():
                     halo(d, 0).wait_recv()
                     halo(d, 1).wait_recv()
+
+            for to in range(2):
+
+                @pl.when((z > 0) & (p == to))
+                def _(to=to):
+                    for source in range(PLANE):
+                        if source == to:
+                            pass_own(source).wait()
+                        else:
+                            pass_copy(source, to).wait_recv()
 
         since = k - first_piece
         piece = jnp.maximum(since, 0) // every
@@ -607,10 +794,20 @@
             part_copy(c, r).wait_send()
     for d in (1, 2):
 
-        @pl.when(me + d <= last)
+        @pl.when(p + d < PLANE)
         def _():
             halo(d, 0).wait_send()
             halo(d, 1).wait_send()
+
+    @pl.when(z < PLANES - 1)
+    def _():
+        edge_copy().wait_send()
+
+    for source in range(PLANE):
+
+        @pl.when((z > 0) & (p == source))
+        def _(source=source):
+            each_pass(source, lambda s, t: pass_copy(s, t).wait_send(), lambda s: None)
 
     for step, into, onward, send, recv, target in (
         (z, ups, ups_out, up_send, up_recv, above),
@@ -632,21 +829,24 @@
                     ).wait_send()
                 return carry
 
-            lax.fori_loop(0, cap_at(step), sent, 0)
-
-
-def attend(caps, group, delay, collective_id, table, gate, q, k, v, gain, *pools):
-    slots = caps[-1]
-    groups = slots // group
+            lax.fori_loop(floor_at(step), cap_at(step), sent, 0)
+
+
+def attend(tier, collective_id, table, gate, q, k, v, gain, *pools):
+    slots = tier[0][-1]
+    groups = slots // tier[1]
     ring = [pltpu.VMEM((slots, ROWS, HD), BF16)] * CHUNKS
     hand = [pltpu.VMEM((PLANE, REQ, ROWS, HD), BF16)] * CHUNKS
     dma = pltpu.SemaphoreType.DMA
     return pl.pallas_call(
-        functools.partial(attend_kernel, caps, group, delay),
+        functools.partial(attend_kernel, tier),
         out_shape=jax.ShapeDtypeStruct((TOK, HEADS_HERE * HD), BF16),
-        in_specs=[SMEM, VMEM, VMEM, ANY, ANY, VMEM] + [ANY] * CHUNKS,
+        in_specs=[SMEM, HBM, HBM, HBM, HBM, HBM] + [pl.BlockSpec(memory_space=pl.ANY)] * (CHUNKS + 1),
         out_specs=VMEM,
         scratch_shapes=[
+            pltpu.VMEM((1, HEADS_HERE), F32),
+            pltpu.VMEM((TOK, HEADS_HERE * HD), BF16),
+            pltpu.VMEM((1, HEADS_HERE * HD), F32),
             pltpu.VMEM((3 * TOK, HEADS_HERE * HD), BF16),
             pltpu.VMEM((3 * TOK, HEADS_HERE * HD), BF16),
             pltpu.VMEM((TOK, HEADS_HERE * HD), F32),
@@ -659,8 +859,9 @@
             *hand,
             pltpu.VMEM((16, HD), F32),
             pltpu.VMEM((8, 16, HD), F32),
+            pltpu.VMEM((2 * TOK, HD), BF16),
             dma((CHUNKS,)),
-            dma((2,)),
+            dma((5,)),
             dma((4,)),
             dma((4,)),
             dma((CHUNKS, groups)),
@@ -671,17 +872,19 @@
             dma((CHUNKS, 8)),
             dma((8,)),
             dma((8,)),
+            dma((2,)),
+            dma((2,)),
+            dma((8,)),
         ],
         compiler_params=pltpu.CompilerParams(
-            collective_id=collective_id, has_side_effects=True, vmem_limit_bytes=48 << 20
+            collective_id=collective_id, has_side_effects=True, vmem_limit_bytes=60 << 20
         ),
         name="attend_" + str(slots),
     )(table, gate, q, k, v, gain, *pools)
 
 
 def shards(queries, keys, values, memory_keys, memory_values, retrieval, gate, gain):
-    *pools, table = spread(retrieval, memory_keys, memory_values)
-    fits = table[1, 4, 0] > 0
+    *pools, edge, table = spread(retrieval, memory_keys, memory_values, keys, values)
     operands = (
         table,
         gate.reshape(1, -1),
@@ -690,11 +893,11 @@
         values,
         gain.reshape(1, -1),
         *pools,
+        edge,
     )
-    return lax.cond(
-        fits,
-        functools.partial(attend, SHORT_CAPS, 8, 2, 1),
-        functools.partial(attend, LONG_CAPS, 16, 2, 2),
+    return lax.switch(
+        table[1, 4, 0],
+        [functools.partial(attend, tier, 1 + i) for i, tier in enumerate(TIERS)],
         *operands,
     )
 

time: 147 us -> 119 us (0.81)
  Pallas kernels: 141 us -> 116 us
  local copies, waits for them, and re-layouts: 4.63 us -> 1.87 us
    pallas_call x1, Pallas kernels: 112 us -> 83.5 us  [attend(): pl.pallas_call(functools.partial(attend_kernel, tier), out_shape=jax.Shap...]
    pallas_call x1, Pallas kernels: 28.6 us -> 32.2 us  [spread(): pl.pallas_call(spread_kernel, out_shape=[jax.ShapeDtypeStruct((LOCAL, ROW...]
    unnamed x17 -> x11, local copies, waits for them, and re-layouts: 4.12 us -> 1.36 us
where the time goes in v2:
time: 119 us
  Pallas kernels  116 us (97%)
  local copies, waits for them, and re-layouts  1.87 us (2%)
    pallas_call x1, Pallas kernels, attend(): pl.pallas_call(functools.partial(attend_kernel, tier), out_shape=jax.Shap...  83.5 us
    pallas_call x1, Pallas kernels, spread(): pl.pallas_call(spread_kernel, out_shape=[jax.ShapeDtypeStruct((LOCAL, ROW...  32.2 us

profile of v2, /device:TPU:1, one launch (start us, length us, event | category | flops | bytes accessed | tf_op | source)
XLA Modules:
  0.0 118.8 jit_solution(12348651652212013777)
XLA Ops:
  0.0 0.0 copy-start
  0.0 0.0 copy-start.1
  0.0 0.0 copy-start.2
  0.0 32.2 %spread_blocks.1 = (bf16[64,32,128]{2,1,0:T(8,128)(2,1)S(1)}, bf16[64,32,128]{2,1,0:T(8,128)(2,1)S(1)}, bf16[512,128]{1,0:T(8,128)(2,1)S(1)}, s32[2,8,128]{2,1,0:T(8,128)S(1)}) custom-call(s32[2,4]{1,0:T(2,128)} %ids_ref.1, bf16[8,64,512]{2,1,0:T(8,128)(2,1)} %mk_ref.1, bf16[8,64,512]{2,1,0:T(8,128)(2,1)} %mv_ref.1, bf16[256,512]{1,0:T(8,128)(2,1)} %k_ref.1, ...), custom_call_target="tpu_custom_call" | custom-call | tf_op jit(solution)/shard_map/spread_blocks/pallas_call | solution.py:379
  32.2 0.5 slice.3
  33.4 0.0 copy-start.3
  33.4 0.0 copy-start.4
  33.4 0.0 copy-done
  33.5 0.0 copy-done.1
  33.5 0.0 copy-done.2
  33.5 0.6 copy-done.3
  34.1 0.0 copy-done.4
  34.1 84.0 %conditional.1 = (bf16[256,512]{1,0:T(8,128)(2,1)S(1)}) conditional(s32[]{:T(128)} %bitcast, (s32[2,8,128]{2,1,0:T(8,128)S(1)}, f32[1,4]{1,0:T(1,128)S(1)}, bf16[256,512]{1,0:T(8,128)(2,1)S(1)}, bf16[256,512]{1,0:T(8,128)(2,1)S(1)}, bf16[256,512]{1,0:T(8,128)(2,1)S(1)}, /*index=5*/f32[1,512]{1,0:T(1,128)S(1)}, ...), branch_computations={%region_0.0_spmd, %region_1.0_spmd, %region_2.0_spmd} | conditional | bytes 8 | solution.py:898
  34.1 83.5 %attend_112.1 = bf16[256,512]{1,0:T(8,128)(2,1)S(1)} custom-call(s32[2,8,128]{2,1,0:T(8,128)S(1)} %get-tuple-element.72.refs_0_, f32[1,4]{1,0:T(1,128)S(1)} %get-tuple-element.73.refs_1_, bf16[256,512]{1,0:T(8,128)(2,1)S(1)} %get-tuple-element.74.refs_2_, bf16[256,512]{1,0:T(8,128)(2,1)S(1)} %get-tuple-element.75.refs_3_, ...), custom_call_target="tpu_custom_call" | custom-call | tf_op jit(solution)/shard_map/cond/branch_1_fun/attend_112/pallas_call | solution.py:841
  118.1 0.7 copy.16
Async XLA Ops:
  0.0 33.4 %copy-start = (bf16[256,512]{1,0:T(8,128)(2,1)S(1)}, bf16[256,512]{1,0:T(8,128)(2,1)}, u32[]{:S(2)}) copy-start(bf16[256,512]{1,0:T(8,128)(2,1)} %k_ref.1) | copy-start | bytes 786436
  0.0 33.4 %copy-start.1 = (bf16[256,512]{1,0:T(8,128)(2,1)S(1)}, bf16[256,512]{1,0:T(8,128)(2,1)}, u32[]{:S(2)}) copy-start(bf16[256,512]{1,0:T(8,128)(2,1)} %v_ref.1) | copy-start | bytes 786436
  0.0 33.5 %copy-start.2 = (bf16[256,512]{1,0:T(8,128)(2,1)S(1)}, bf16[256,512]{1,0:T(8,128)(2,1)}, u32[]{:S(2)}) copy-start(bf16[256,512]{1,0:T(8,128)(2,1)} %param.11) | copy-start | bytes 786436
  33.4 0.7 copy-start.3
  33.4 0.7 copy-start.4

commit v3 on v2

--- a/solution.py
+++ b/solution.py
@@ -23,17 +23,13 @@
 REQ = 8
 BLK = 64
 LOCAL = 64
-SLOTS = 256
 TOK = 256
 CHUNKS = 2
 ROWS = BLK // CHUNKS
 SCALE = 1.0 / math.sqrt(HD)
 
-TIERS = (
-    ((48, 80, 96, 104), 8, (3, 7, 10, 11), 16),
-    ((56, 88, 104, 112), 8, (3, 7, 10, 11), 16),
-    ((64, 128, 192, 256), 16, (2, 4, 6, 8), 0),
-)
+SHORT = ((56, 88, 104, 112), 8, (3, 7, 10, 11), 16, 128)
+LONG = ((64, 128, 192, 256), 16, (2, 4, 6, 8), 0, 256)
 REACHES = (7, 1, 2, 3, 4, 5, 6)
 
 
@@ -58,7 +54,8 @@
     pl.semaphore_wait(barrier, total)
 
 
-def schedule(lists, my_z, table_ref):
+def schedule(tier, lists, my_z, table_ref):
+    caps, _, _, left_out, known = tier
     block = iota((1, PLANES * LOCAL), 1)
     asker_z = jnp.floor(iota((PLANES * PLANE, 1), 0) / PLANE)
     top = jnp.full((1, PLANES * LOCAL), -1.0, F32)
@@ -68,21 +65,21 @@
         top = jnp.maximum(top, jnp.max(jnp.where(hit, asker_z, -1.0), axis=0, keepdims=True))
         low = jnp.minimum(low, jnp.min(jnp.where(hit, asker_z, 8.0), axis=0, keepdims=True))
     before_lane = (iota((LOCAL, LOCAL), 0) < iota((LOCAL, LOCAL), 1)).astype(BF16)
-    after_row = (iota((SLOTS, SLOTS), 1) > iota((SLOTS, SLOTS), 0)).astype(BF16)
+    after_row = (iota((known, known), 1) > iota((known, known), 0)).astype(BF16)
     before_kind = (iota((8, 8), 1) < iota((8, 8), 0)).astype(BF16)
-    slot_column = iota((SLOTS, 1), 0)
+    slot_column = iota((known, 1), 0)
     kind = jnp.full((8, 1), -1.0, F32)
     for i, reach in enumerate(REACHES):
         kind = jnp.where(iota((8, 1), 0) == i, reach, kind)
     lane = iota((1, LOCAL), 1)
-    fits = [jnp.ones((1, 1), F32) for _ in TIERS[:-1]]
+    fits = jnp.ones((1, 1), F32)
     injected, arrived = [], []
     for up in (True, False):
         height = jnp.zeros((1, 1), F32)
-        end = jnp.full((SLOTS, 1), -1.0, F32)
-        held = jnp.full((SLOTS, 1), -1.0, F32)
-        mine_in = jnp.full((SLOTS, 1), -1.0, F32)
-        mine_arrived = jnp.full((SLOTS, 1), -1.0, F32)
+        end = jnp.full((known, 1), -1.0, F32)
+        held = jnp.full((known, 1), -1.0, F32)
+        mine_in = jnp.full((known, 1), -1.0, F32)
+        mine_arrived = jnp.full((known, 1), -1.0, F32)
         for step in range(PLANES - 1):
             z = step if up else PLANES - 1 - step
             reach = top[:, z * LOCAL : (z + 1) * LOCAL]
@@ -103,7 +100,7 @@
             height = jnp.maximum(height, load)
             free = ((end <= step) & (slot_column < height)).astype(F32)
             free_rank = jnp.dot(
-                after_row, jnp.broadcast_to(free, (SLOTS, HD)).astype(BF16), preferred_element_type=F32
+                after_row, jnp.broadcast_to(free, (known, HD)).astype(BF16), preferred_element_type=F32
             )[:, 0:1]
             pair = (free_rank == fresh_rank) & (free > 0.5) & (fresh > 0.5)
             code = jnp.sum(jnp.where(pair, 1.0 + lane + LOCAL * reach, 0.0), axis=1, keepdims=True)
@@ -113,22 +110,17 @@
             inject = jnp.where(taken, new_block, -1.0)
             held = jnp.where(taken, z * LOCAL + new_block, jnp.where(end <= step, -1.0, held))
             end = jnp.where(taken, new_end, end)
-            fits = [
-                fit * (load <= tier[0][min(step, 3)]).astype(F32)
-                for fit, tier in zip(fits, TIERS)
-            ]
+            fits = fits * (load <= caps[min(step, 3)]).astype(F32)
             if step == PLANES - 2:
                 lowest = jnp.min(
-                    jnp.where(end > step, slot_column, SLOTS), axis=0, keepdims=True
+                    jnp.where(end > step, slot_column, known), axis=0, keepdims=True
                 )
-                fits = [
-                    fit * (lowest >= tier[3]).astype(F32) for fit, tier in zip(fits, TIERS)
-                ]
+                fits = fits * (lowest >= left_out).astype(F32)
             mine_in = jnp.where(my_z == z, inject, mine_in)
             mine_arrived = jnp.where(my_z == (z + 1 if up else z - 1), held, mine_arrived)
         injected.append(mine_in)
         arrived.append(mine_arrived)
-    diagonal = iota((SLOTS, SLOTS), 0) == iota((SLOTS, SLOTS), 1)
+    diagonal = iota((known, known), 0) == iota((known, known), 1)
 
     def as_row(column):
         return jnp.sum(jnp.where(diagonal, column, 0.0), axis=0, keepdims=True)
@@ -136,14 +128,13 @@
     in_up, in_down = as_row(injected[0]), as_row(injected[1])
     at_up, at_down = as_row(arrived[0]), as_row(arrived[1])
     rows = iota((8, HD), 0)
-    out = jnp.where(rows == 0, in_up[:, :HD], 0.0)
-    out = jnp.where(rows == 1, in_up[:, HD:], out)
-    out = jnp.where(rows == 2, in_down[:, :HD], out)
-    out = jnp.where(rows == 3, in_down[:, HD:], out)
-    out = jnp.where(rows == 4, len(fits) - sum(fits), out)
+    out = jnp.where(rows == 4, fits, 0.0)
+    for i in range(known // HD):
+        out = jnp.where(rows == i, in_up[:, i * HD : (i + 1) * HD], out)
+        out = jnp.where(rows == 2 + i, in_down[:, i * HD : (i + 1) * HD], out)
     table_ref[1] = out.astype(jnp.int32)
 
-    slot = iota((1, SLOTS), 1)
+    slot = iota((1, known), 1)
     mine = jnp.zeros((PLANE, HD), F32)
     for z in range(PLANES):
         mine = jnp.where(my_z == z, lists[z * PLANE : (z + 1) * PLANE], mine)
@@ -155,276 +146,32 @@
         owner_z = jnp.floor(wanted / LOCAL)
         slot_up = jnp.sum(jnp.where(at_up == wanted, slot, 0.0), axis=1, keepdims=True)
         slot_down = jnp.sum(jnp.where(at_down == wanted, slot, 0.0), axis=1, keepdims=True)
-        found = jnp.where(owner_z == z_here, wanted - LOCAL * owner_z, LOCAL + SLOTS + slot_down)
+        found = jnp.where(owner_z == z_here, wanted - LOCAL * owner_z, LOCAL + known + slot_down)
         found = jnp.where(owner_z < z_here, LOCAL + slot_up, found)
         place = jnp.where(lanes == j, found, place)
     table_ref[0] = place.astype(jnp.int32)
 
 
-def spread_kernel(
-    ids_ref, mk_ref, mv_ref, k_ref, v_ref, *rest
-):
-    pools = rest[:CHUNKS]
-    (
-        edge_ref,
-        table_ref,
-        line,
-        lists,
-        send1,
-        recv1,
-        send2,
-        recv2,
-        send_a,
-        recv_a,
-        own_sem,
-        edge_send,
-        edge_recv,
-    ) = rest[CHUNKS:]
-    me = lax.axis_index("ctx")
-    z, p = me // PLANE, me % PLANE
-    x, core = p // 2, p % 2
-
-    def in_plane(r):
-        return {"ctx": z * PLANE + (p + r) % PLANE}
-
-    def on_line(r):
-        return {"ctx": ((z + r) % PLANES) * PLANE + p}
-
-    greet([(in_plane(r), None) for r in range(1, 8)] + [(on_line(r), None) for r in range(1, 8)])
-
-    lanes = lax.broadcasted_iota(jnp.int32, (8, HD), 1)
-    row = jnp.zeros((8, HD), jnp.int32)
-    for j in range(REQ):
-        row = jnp.where(lanes == j, ids_ref[j // 4, j % 4], row)
-    line[p] = row
-
-    def copy1(r):
-        return pltpu.make_async_remote_copy(
-            src_ref=line.at[p],
-            dst_ref=line.at[p],
-            send_sem=send1.at[r],
-            recv_sem=recv1.at[p],
-            device_id=in_plane(r),
-            device_id_type=MESH,
-        )
-
-    def arrival1(r):
-        q = (p + r) % PLANE
-        return pltpu.make_async_remote_copy(
-            src_ref=line.at[q],
-            dst_ref=line.at[q],
-            send_sem=send1.at[r],
-            recv_sem=recv1.at[q],
-            device_id=in_plane(r),
-            device_id_type=MESH,
-        )
-
-    for r in range(1, 8):
-        copy1(r).start()
-
-    def part(r, chunk, ref):
-        q = (p + r) % PLANE
-        return ref.at[:, pl.ds(chunk * ROWS, ROWS), pl.ds(pl.multiple_of((q // 2) * HD, HD), HD)]
-
-    def copy_a(r, chunk, ref):
-        return pltpu.make_async_remote_copy(
-            src_ref=part(r, chunk, ref),
-            dst_ref=pools[chunk].at[pl.ds(p * 8, 8)],
-            send_sem=send_a.at[chunk, r],
-            recv_sem=recv_a.at[chunk, p],
-            device_id=in_plane(r),
-            device_id_type=MESH,
-        )
-
-    def arrival_a(r, chunk):
-        q = (p + r) % PLANE
-        return pltpu.make_async_remote_copy(
-            src_ref=part(r, chunk, mk_ref),
-            dst_ref=pools[chunk].at[pl.ds(q * 8, 8)],
-            send_sem=send_a.at[chunk, r],
-            recv_sem=recv_a.at[chunk, q],
-            device_id=in_plane(r),
-            device_id_type=MESH,
-        )
-
-    for chunk in range(CHUNKS):
-        for r in (4, 3, 5, 2, 6, 1, 7):
-            to_core = (core + r) % 2
-
-            @pl.when(to_core == 0)
-            def _():
-                copy_a(r, chunk, mk_ref).start()
-
-            @pl.when(to_core == 1)
-            def _():
-                copy_a(r, chunk, mv_ref).start()
-
-        def own(ref, chunk=chunk):
-            return pltpu.make_async_copy(
-                part(0, chunk, ref), pools[chunk].at[pl.ds(p * 8, 8)], own_sem.at[chunk]
-            )
-
-        @pl.when(core == 0)
-        def _():
-            own(mk_ref).start()
-
-        @pl.when(core == 1)
-        def _():
-            own(mv_ref).start()
-
-    def edge_part(q):
-        ref = v_ref if q % 2 else k_ref
-        return ref.at[:, pl.ds(q // 2 * HD, HD)]
-
-    def edge_copy(q):
-        return pltpu.make_async_remote_copy(
-            src_ref=edge_part(q),
-            dst_ref=edge_ref.at[pl.ds(core * TOK, TOK)],
-            send_sem=edge_send.at[q],
-            recv_sem=edge_recv.at[core],
-            device_id={"ctx": z * PLANE + q},
-            device_id_type=MESH,
-        )
-
-    def edge_arrival(source):
-        return pltpu.make_async_remote_copy(
-            src_ref=edge_part(0),
-            dst_ref=edge_ref.at[pl.ds(source * TOK, TOK)],
-            send_sem=edge_send.at[0],
-            recv_sem=edge_recv.at[source],
-            device_id=in_plane(1),
-            device_id_type=MESH,
-        )
-
-    def edge_own(q):
-        return pltpu.make_async_copy(
-            edge_part(q), edge_ref.at[pl.ds(core * TOK, TOK)], own_sem.at[CHUNKS]
-        )
-
-    sends_edge = (x == 3) & (z < PLANES - 1)
-    for q in range(PLANE):
-
-        @pl.when(sends_edge & (p != q))
-        def _(q=q):
-            edge_copy(q).start()
-
-        @pl.when(sends_edge & (p == q))
-        def _(q=q):
-            edge_own(q).start()
-
-    for r in range(1, 8):
-        arrival1(r).wait_recv()
-    rows = lax.broadcasted_iota(jnp.int32, (8, HD), 0)
-    whole = jnp.zeros((8, HD), jnp.int32)
-    for q in range(PLANE):
-        whole = jnp.where(rows == q, line[q], whole)
-    lists[z] = whole
-
-    def copy2(r):
-        return pltpu.make_async_remote_copy(
-            src_ref=lists.at[z],
-            dst_ref=lists.at[z],
-            send_sem=send2.at[r],
-            recv_sem=recv2.at[z],
-            device_id=on_line(r),
-            device_id_type=MESH,
-        )
-
-    def arrival2(r):
-        q = (z + r) % PLANES
-        return pltpu.make_async_remote_copy(
-            src_ref=lists.at[q],
-            dst_ref=lists.at[q],
-            send_sem=send2.at[r],
-            recv_sem=recv2.at[q],
-            device_id=on_line(r),
-            device_id_type=MESH,
-        )
-
-    for r in range(1, 8):
-        copy2(r).start()
-    for r in range(1, 8):
-        arrival2(r).wait_recv()
-    schedule(lists[...].reshape(PLANES * PLANE, HD).astype(F32), z, table_ref)
-
-    for r in range(1, 8):
-        copy1(r).wait_send()
-        copy2(r).wait_send()
-    for q in range(PLANE):
-
-        @pl.when(sends_edge & (p != q))
-        def _(q=q):
-            edge_copy(q).wait_send()
-
-        @pl.when(sends_edge & (p == q))
-        def _(q=q):
-            edge_own(q).wait()
-
-    for source in range(2):
-
-        @pl.when((z < PLANES - 1) & (p != 6 + source))
-        def _(source=source):
-            edge_arrival(source).wait_recv()
-
-    for chunk in range(CHUNKS):
-        pltpu.make_async_copy(
-            part(0, chunk, mk_ref), pools[chunk].at[pl.ds(p * 8, 8)], own_sem.at[chunk]
-        ).wait()
-        for r in range(1, 8):
-            copy_a(r, chunk, mk_ref).wait_send()
-            arrival_a(r, chunk).wait_recv()
-
-
-def spread(retrieval, mk, mv, k, v):
-    return pl.pallas_call(
-        spread_kernel,
-        out_shape=[jax.ShapeDtypeStruct((LOCAL, ROWS, HD), BF16)] * CHUNKS
-        + [
-            jax.ShapeDtypeStruct((2 * TOK, HD), BF16),
-            jax.ShapeDtypeStruct((2, 8, HD), jnp.int32),
-        ],
-        in_specs=[SMEM, HBM, HBM, HBM, HBM],
-        out_specs=[pl.BlockSpec(memory_space=pl.ANY)] * (CHUNKS + 1) + [VMEM],
-        scratch_shapes=[
-            pltpu.VMEM((PLANE, 8, HD), jnp.int32),
-            pltpu.VMEM((PLANES, 8, HD), jnp.int32),
-            pltpu.SemaphoreType.DMA((8,)),
-            pltpu.SemaphoreType.DMA((8,)),
-            pltpu.SemaphoreType.DMA((8,)),
-            pltpu.SemaphoreType.DMA((8,)),
-            pltpu.SemaphoreType.DMA((CHUNKS, 8)),
-            pltpu.SemaphoreType.DMA((CHUNKS, 8)),
-            pltpu.SemaphoreType.DMA((CHUNKS + 1,)),
-            pltpu.SemaphoreType.DMA((8,)),
-            pltpu.SemaphoreType.DMA((2,)),
-        ],
-        compiler_params=pltpu.CompilerParams(
-            collective_id=0, has_side_effects=True, vmem_limit_bytes=62 << 20
-        ),
-        name="spread_blocks",
-    )(retrieval, mk, mv, k, v)
-
-
 def attend_kernel(tier, *refs):
-    caps, group, lags, left_out = tier
+    caps, group, lags, left_out, known = tier
     slots = caps[-1]
     groups = slots // group
-    table, gate_hbm, q_hbm, k_ref, v_ref, gain_hbm = refs[:6]
-    rest = list(refs[6:])
+    ids_ref, gate_hbm, gain_hbm, q_hbm, k_ref, v_ref, mk_ref, mv_ref = refs[:8]
+    out_ref, fits_ref = refs[8:10]
+    rest = list(refs[10:])
 
     def take(n):
         got = rest[:n]
         del rest[:n]
         return got
 
-    given = take(CHUNKS)
-    (edge_ref,) = take(1)
-    (out_ref,) = take(1)
+    table_out, table, line, lists = take(4)
     gate_ref, q_ref, gain_ref, near_k, near_v, mixed = take(6)
     pools, ups, downs = take(CHUNKS), take(CHUNKS), take(CHUNKS)
     ups_out, downs_out = take(CHUNKS), take(CHUNKS)
     parts_out, parts = take(CHUNKS), take(CHUNKS)
-    squares_out, squares, edge_in = take(3)
+    squares_out, squares, edge_ref, edge_in = take(4)
+    table_sem, send1, recv1, send2, recv2, send_a, recv_a, edge_send, edge_recv = take(9)
     (
         pool_sem,
         own_sem,
@@ -446,17 +193,19 @@
     me = lax.axis_index("ctx")
     mem = lax.axis_index("mem")
     z, p = me // PLANE, me % PLANE
+    x, core = p // 2, p % 2
 
     def in_plane(r):
         return {"ctx": z * PLANE + (p + r) % PLANE}
 
+    def on_line(r):
+        return {"ctx": ((z + r) % PLANES) * PLANE + p}
+
     def mem_peer(r):
         return {"mem": (mem + r) % 8}
 
     above, below = {"ctx": me + PLANE}, {"ctx": me - PLANE}
     loads = [
-        pltpu.make_async_copy(given[c], pools[c], pool_sem.at[c]) for c in range(CHUNKS)
-    ] + [
         pltpu.make_async_copy(k_ref, near_k.at[pl.ds(2 * TOK, TOK)], own_sem.at[0]),
         pltpu.make_async_copy(v_ref, near_v.at[pl.ds(2 * TOK, TOK)], own_sem.at[1]),
         pltpu.make_async_copy(q_hbm, q_ref, own_sem.at[2]),
@@ -469,7 +218,7 @@
     greet(
         [(in_plane(r), None) for r in range(1, 8)]
         + [(mem_peer(r), None) for r in range(1, 8)]
-        + [(above, z < PLANES - 1), (below, z > 0)]
+        + [(on_line(r), None) for r in range(1, 8)]
     )
 
     def edge_copy():
@@ -482,9 +231,20 @@
             device_id_type=MESH,
         )
 
-    @pl.when(z < PLANES - 1)
-    def _():
-        edge_copy().start()
+    def edge_here():
+        for source in range(2):
+
+            @pl.when((z < PLANES - 1) & (p == 6 + source))
+            def _(source=source):
+                edge_own(0).wait()
+
+            @pl.when((z < PLANES - 1) & (p != 6 + source))
+            def _(source=source):
+                edge_arrival(source).wait_recv()
+
+        @pl.when(z < PLANES - 1)
+        def _():
+            edge_copy().start()
 
     def passed(source, to):
         near = near_v if source % 2 else near_k
@@ -526,6 +286,135 @@
                     lambda s: pass_own(s).start(),
                 )
 
+    lanes = lax.broadcasted_iota(jnp.int32, (8, HD), 1)
+    row = jnp.zeros((8, HD), jnp.int32)
+    for j in range(REQ):
+        row = jnp.where(lanes == j, ids_ref[j // 4, j % 4], row)
+    line[p] = row
+
+    def copy1(r):
+        return pltpu.make_async_remote_copy(
+            src_ref=line.at[p],
+            dst_ref=line.at[p],
+            send_sem=send1.at[r],
+            recv_sem=recv1.at[p],
+            device_id=in_plane(r),
+            device_id_type=MESH,
+        )
+
+    def arrival1(r):
+        q = (p + r) % PLANE
+        return pltpu.make_async_remote_copy(
+            src_ref=line.at[q],
+            dst_ref=line.at[q],
+            send_sem=send1.at[r],
+            recv_sem=recv1.at[q],
+            device_id=in_plane(r),
+            device_id_type=MESH,
+        )
+
+    for r in range(1, 8):
+        copy1(r).start()
+
+    def part(r, chunk, ref):
+        q = (p + r) % PLANE
+        return ref.at[:, pl.ds(chunk * ROWS, ROWS), pl.ds(pl.multiple_of((q // 2) * HD, HD), HD)]
+
+    def copy_a(r, chunk, ref):
+        return pltpu.make_async_remote_copy(
+            src_ref=part(r, chunk, ref),
+            dst_ref=pools[chunk].at[pl.ds(p * 8, 8)],
+            send_sem=send_a.at[chunk, r],
+            recv_sem=recv_a.at[chunk, p],
+            device_id=in_plane(r),
+            device_id_type=MESH,
+        )
+
+    def arrival_a(r, chunk):
+        q = (p + r) % PLANE
+        return pltpu.make_async_remote_copy(
+            src_ref=part(r, chunk, mk_ref),
+            dst_ref=pools[chunk].at[pl.ds(q * 8, 8)],
+            send_sem=send_a.at[chunk, r],
+            recv_sem=recv_a.at[chunk, q],
+            device_id=in_plane(r),
+            device_id_type=MESH,
+        )
+
+    def own_a(ref, chunk):
+        return pltpu.make_async_copy(
+            part(0, chunk, ref), pools[chunk].at[pl.ds(p * 8, 8)], pool_sem.at[chunk]
+        )
+
+    def spread_blocks(chunk):
+        for r in (4, 3, 5, 2, 6, 1, 7):
+            to_core = (core + r) % 2
+
+            @pl.when(to_core == 0)
+            def _():
+                copy_a(r, chunk, mk_ref).start()
+
+            @pl.when(to_core == 1)
+            def _():
+                copy_a(r, chunk, mv_ref).start()
+
+        @pl.when(core == 0)
+        def _():
+            own_a(mk_ref, chunk).start()
+
+        @pl.when(core == 1)
+        def _():
+            own_a(mv_ref, chunk).start()
+
+    def blocks_here(chunk):
+        own_a(mk_ref, chunk).wait()
+        for r in range(1, 8):
+            arrival_a(r, chunk).wait_recv()
+
+    spread_blocks(0)
+
+    def edge_part(q):
+        ref = v_ref if q % 2 else k_ref
+        return ref.at[:, pl.ds(q // 2 * HD, HD)]
+
+    def spread_edge(q):
+        return pltpu.make_async_remote_copy(
+            src_ref=edge_part(q),
+            dst_ref=edge_ref.at[pl.ds(core * TOK, TOK)],
+            send_sem=edge_send.at[q],
+            recv_sem=edge_recv.at[core],
+            device_id={"ctx": z * PLANE + q},
+            device_id_type=MESH,
+        )
+
+    def edge_arrival(source):
+        return pltpu.make_async_remote_copy(
+            src_ref=edge_part(0),
+            dst_ref=edge_ref.at[pl.ds(source * TOK, TOK)],
+            send_sem=edge_send.at[0],
+            recv_sem=edge_recv.at[source],
+            device_id=in_plane(1),
+            device_id_type=MESH,
+        )
+
+    def edge_own(q):
+        return pltpu.make_async_copy(
+            edge_part(q), edge_ref.at[pl.ds(core * TOK, TOK)], pool_sem.at[CHUNKS]
+        )
+
+    sends_edge = (x == 3) & (z < PLANES - 1)
+    for q in range(PLANE):
+
+        @pl.when(sends_edge & (p != q))
+        def _(q=q):
+            spread_edge(q).start()
+
+        @pl.when(sends_edge & (p == q))
+        def _(q=q):
+            edge_own(q).start()
+
+    for chunk in range(1, CHUNKS):
+        spread_blocks(chunk)
     def halo(d, which):
         ref, near = ((k_ref, near_k), (v_ref, near_v))[which]
         return pltpu.make_async_remote_copy(
@@ -549,8 +438,48 @@
             near_k[pl.ds((2 - d) * TOK, TOK)] = jnp.zeros((TOK, HEADS_HERE * HD), BF16)
             near_v[pl.ds((2 - d) * TOK, TOK)] = jnp.zeros((TOK, HEADS_HERE * HD), BF16)
 
+    for r in range(1, 8):
+        arrival1(r).wait_recv()
+    rows = lax.broadcasted_iota(jnp.int32, (8, HD), 0)
+    whole = jnp.zeros((8, HD), jnp.int32)
+    for q in range(PLANE):
+        whole = jnp.where(rows == q, line[q], whole)
+    lists[z] = whole
+
+    def copy2(r):
+        return pltpu.make_async_remote_copy(
+            src_ref=lists.at[z],
+            dst_ref=lists.at[z],
+            send_sem=send2.at[r],
+            recv_sem=recv2.at[z],
+            device_id=on_line(r),
+            device_id_type=MESH,
+        )
+
+    def arrival2(r):
+        q = (z + r) % PLANES
+        return pltpu.make_async_remote_copy(
+            src_ref=lists.at[q],
+            dst_ref=lists.at[q],
+            send_sem=send2.at[r],
+            recv_sem=recv2.at[q],
+            device_id=on_line(r),
+            device_id_type=MESH,
+        )
+
+    for r in range(1, 8):
+        copy2(r).start()
+    for r in range(1, 8):
+        arrival2(r).wait_recv()
+    schedule(tier, lists[...].reshape(PLANES * PLANE, HD).astype(F32), z, table_out)
+    to_scalars = pltpu.make_async_copy(table_out, table, table_sem)
+    to_scalars.start()
+    to_scalars.wait()
+    fits_ref[0] = table[1, 4, 0]
+    edge_here()
     for load in loads:
         load.wait()
+    blocks_here(0)
 
     caps_g = [c // group for c in caps]
 
@@ -603,7 +532,7 @@
                     for i in range(group):
                         slot = g * group + i
                         inject = table[1, row + slot // HD, slot % HD]
-                        local = pool[c][jnp.maximum(inject, 0)]
+                        local = pool[c][jnp.clip(inject, 0, LOCAL - 1)]
                         onward[c][slot] = jnp.where(inject >= 0, local, into[c][slot])
                     copy(c).start()
 
@@ -632,11 +561,11 @@
     def hand_out(c):
         def pick(q, j):
             place = table[0, q, j]
-            own = pools[c][jnp.minimum(place, LOCAL - 1)]
+            own = pools[c][jnp.clip(place, 0, LOCAL - 1)]
             from_below = ups[c][jnp.clip(place - LOCAL, 0, slots - 1)]
-            from_above = downs[c][jnp.clip(place - LOCAL - SLOTS, 0, slots - 1)]
+            from_above = downs[c][jnp.clip(place - LOCAL - known, 0, slots - 1)]
             return jnp.where(
-                place < LOCAL, own, jnp.where(place < LOCAL + SLOTS, from_below, from_above)
+                place < LOCAL, own, jnp.where(place < LOCAL + known, from_below, from_above)
             )
 
         for r in (4, 3, 5, 2, 6, 1, 7):
@@ -676,6 +605,12 @@
     first_piece = steps - 4 - every * pieces
 
     def step_body(k, carry):
+        for chunk in range(1, CHUNKS):
+
+            @pl.when(k == (chunk - 1) * groups + caps_g[0])
+            def _(chunk=chunk):
+                blocks_here(chunk)
+
         conveyor(k, z, above, pools, ups, ups_out, up_send, up_recv, 0)
         conveyor(k, PLANES - 1 - z, below, pools, downs, downs_out, down_send, down_recv, 2)
         for c in range(CHUNKS):
@@ -792,6 +727,16 @@
         square_copy(r).wait_send()
         for c in range(CHUNKS):
             part_copy(c, r).wait_send()
+        copy1(r).wait_send()
+        copy2(r).wait_send()
+        for chunk in range(CHUNKS):
+            copy_a(r, chunk, mk_ref).wait_send()
+    for q in range(PLANE):
+
+        @pl.when(sends_edge & (p != q))
+        def _(q=q):
+            spread_edge(q).wait_send()
+
     for d in (1, 2):
 
         @pl.when(p + d < PLANE)
@@ -832,7 +777,7 @@
             lax.fori_loop(floor_at(step), cap_at(step), sent, 0)
 
 
-def attend(tier, collective_id, table, gate, q, k, v, gain, *pools):
+def attend(tier, collective_id, ids, gate, gain, q, k, v, mk, mv):
     slots = tier[0][-1]
     groups = slots // tier[1]
     ring = [pltpu.VMEM((slots, ROWS, HD), BF16)] * CHUNKS
@@ -840,10 +785,17 @@
     dma = pltpu.SemaphoreType.DMA
     return pl.pallas_call(
         functools.partial(attend_kernel, tier),
-        out_shape=jax.ShapeDtypeStruct((TOK, HEADS_HERE * HD), BF16),
-        in_specs=[SMEM, HBM, HBM, HBM, HBM, HBM] + [pl.BlockSpec(memory_space=pl.ANY)] * (CHUNKS + 1),
-        out_specs=VMEM,
+        out_shape=[
+            jax.ShapeDtypeStruct((TOK, HEADS_HERE * HD), BF16),
+            jax.ShapeDtypeStruct((1,), jnp.int32),
+        ],
+        in_specs=[SMEM] + [HBM] * 7,
+        out_specs=[VMEM, SMEM],
         scratch_shapes=[
+            pltpu.VMEM((2, 8, HD), jnp.int32),
+            pltpu.SMEM((2, 8, HD), jnp.int32),
+            pltpu.VMEM((PLANE, 8, HD), jnp.int32),
+            pltpu.VMEM((PLANES, 8, HD), jnp.int32),
             pltpu.VMEM((1, HEADS_HERE), F32),
             pltpu.VMEM((TOK, HEADS_HERE * HD), BF16),
             pltpu.VMEM((1, HEADS_HERE * HD), F32),
@@ -860,7 +812,17 @@
             pltpu.VMEM((16, HD), F32),
             pltpu.VMEM((8, 16, HD), F32),
             pltpu.VMEM((2 * TOK, HD), BF16),
-            dma((CHUNKS,)),
+            pltpu.VMEM((2 * TOK, HD), BF16),
+            dma(()),
+            dma((8,)),
+            dma((8,)),
+            dma((8,)),
+            dma((8,)),
+            dma((CHUNKS, 8)),
+            dma((CHUNKS, 8)),
+            dma((8,)),
+            dma((2,)),
+            dma((CHUNKS + 1,)),
             dma((5,)),
             dma((4,)),
             dma((4,)),
@@ -880,24 +842,26 @@
             collective_id=collective_id, has_side_effects=True, vmem_limit_bytes=60 << 20
         ),
         name="attend_" + str(slots),
-    )(table, gate, q, k, v, gain, *pools)
+    )(ids, gate, gain, q, k, v, mk, mv)
 
 
 def shards(queries, keys, values, memory_keys, memory_values, retrieval, gate, gain):
-    *pools, edge, table = spread(retrieval, memory_keys, memory_values, keys, values)
     operands = (
-        table,
+        retrieval,
         gate.reshape(1, -1),
+        gain.reshape(1, -1),
         queries,
         keys,
         values,
-        gain.reshape(1, -1),
-        *pools,
-        edge,
+        memory_keys,
+        memory_values,
     )
-    return lax.switch(
-        table[1, 4, 0],
-        [functools.partial(attend, tier, 1 + i) for i, tier in enumerate(TIERS)],
+    out, fits = attend(SHORT, 0, *operands)
+    return lax.cond(
+        fits[0] > 0,
+        lambda out, *_: out,
+        lambda _, *operands: attend(LONG, 1, *operands)[0],
+        out,
         *operands,
     )
 

time: 119 us -> 111 us (0.933)
  Pallas kernels: 116 us -> 108 us
    pallas_call x2 -> x1, Pallas kernels: 116 us -> 108 us  [attend(): pl.pallas_call(functools.partial(attend_kernel, tier), out_shape=[jax.Sha...]
where the time goes in v3:
time: 111 us; the launch traced here: 110 us
  Pallas kernels  108 us (97%)
  local copies, waits for them, and re-layouts  1.42 us (1%)
    pallas_call x1, Pallas kernels, attend(): pl.pallas_call(functools.partial(attend_kernel, tier), out_shape=[jax.Sha...  108 us

profile of v3, /device:TPU:1, one launch (start us, length us, event | category | flops | bytes accessed | tf_op | source)
XLA Modules:
  0.0 110.4 jit_solution(7809082918140779777)
XLA Ops:
  0.0 0.0 copy-start.5
  0.0 0.0 copy-start.6
  0.0 0.0 copy-start.7
  0.0 0.7 copy-done.5
  0.7 0.0 copy-done.6
  0.7 0.0 copy-done.7
  0.7 0.0 copy-start
  0.7 0.0 copy-start.1
  0.7 0.0 copy-start.2
  0.7 0.0 copy-start.3
  0.7 0.0 copy-start.4
  0.7 108.0 %attend_112.1 = (bf16[256,512]{1,0:T(8,128)(2,1)S(1)}, s32[1]{0:T(128)}) custom-call(s32[2,4]{1,0:T(2,128)S(1)} %copy-done.6, f32[1,4]{1,0:T(1,128)S(1)} %bitcast.5, f32[1,512]{1,0:T(1,128)S(1)} %bitcast.3, bf16[256,512]{1,0:T(8,128)(2,1)} %refs_3_.1, bf16[256,512]{1,0:T(8,128)(2,1)} %refs_4_.1, bf16[256,512]{1,0:T(8,128)(2,1)} %refs_5_.1, ...), custom_call_target="tpu_custom_call" | custom-call | tf_op jit(solution)/shard_map/attend_112/pallas_call | solution.py:786
  109.4 0.0 copy-done
  109.4 0.0 copy-done.1
  109.4 0.0 copy-done.2
  109.4 0.0 copy-done.3
  109.4 0.0 copy-done.4
  109.4 0.2 conditional.1
  109.7 0.7 copy.14
Async XLA Ops:
  0.0 0.7 copy-start.5
  0.0 0.7 copy-start.6
  0.0 0.7 copy-start.7
  0.7 108.7 %copy-start = (bf16[8,64,512]{2,1,0:T(8,128)(2,1)S(1)}, bf16[8,64,512]{2,1,0:T(8,128)(2,1)}, u32[]{:S(2)}) copy-start(bf16[8,64,512]{2,1,0:T(8,128)(2,1)} %refs_6_.1) | copy-start | bytes 1572868
  0.7 108.7 %copy-start.1 = (bf16[8,64,512]{2,1,0:T(8,128)(2,1)S(1)}, bf16[8,64,512]{2,1,0:T(8,128)(2,1)}, u32[]{:S(2)}) copy-start(bf16[8,64,512]{2,1,0:T(8,128)(2,1)} %refs_7_.1) | copy-start | bytes 1572868
  0.7 108.7 %copy-start.2 = (bf16[256,512]{1,0:T(8,128)(2,1)S(1)}, bf16[256,512]{1,0:T(8,128)(2,1)}, u32[]{:S(2)}) copy-start(bf16[256,512]{1,0:T(8,128)(2,1)} %refs_3_.1) | copy-start | bytes 786436
  0.7 108.7 %copy-start.3 = (bf16[256,512]{1,0:T(8,128)(2,1)S(1)}, bf16[256,512]{1,0:T(8,128)(2,1)}, u32[]{:S(2)}) copy-start(bf16[256,512]{1,0:T(8,128)(2,1)} %refs_4_.1) | copy-start | bytes 786436
  0.7 108.7 %copy-start.4 = (bf16[256,512]{1,0:T(8,128)(2,1)S(1)}, bf16[256,512]{1,0:T(8,128)(2,1)}, u32[]{:S(2)}) copy-start(bf16[256,512]{1,0:T(8,128)(2,1)} %refs_5_.1) | copy-start | bytes 786436

commit v4 on v3

--- a/solution.py
+++ b/solution.py
@@ -64,69 +64,113 @@
         hit = lists[:, j : j + 1] == block
         top = jnp.maximum(top, jnp.max(jnp.where(hit, asker_z, -1.0), axis=0, keepdims=True))
         low = jnp.minimum(low, jnp.min(jnp.where(hit, asker_z, 8.0), axis=0, keepdims=True))
-    before_lane = (iota((LOCAL, LOCAL), 0) < iota((LOCAL, LOCAL), 1)).astype(BF16)
-    after_row = (iota((known, known), 1) > iota((known, known), 0)).astype(BF16)
-    before_kind = (iota((8, 8), 1) < iota((8, 8), 0)).astype(BF16)
-    slot_column = iota((known, 1), 0)
     kind = jnp.full((8, 1), -1.0, F32)
     for i, reach in enumerate(REACHES):
         kind = jnp.where(iota((8, 1), 0) == i, reach, kind)
-    lane = iota((1, LOCAL), 1)
+    turns = [(way, step) for step in range(PLANES - 1) for way in range(2)]
+
+    def plane(way, step):
+        return step if way == 0 else PLANES - 1 - step
+
+    reaches = {}
+    for way in range(2):
+        for step in range(PLANES):
+            z = plane(way, step)
+            span = slice(z * LOCAL, (z + 1) * LOCAL)
+            reaches[way, step] = top[:, span] if way == 0 else (PLANES - 1) - low[:, span]
+    stacked = [
+        jnp.concatenate([reaches[way, step] for step in range(PLANES)], axis=0) for way in range(2)
+    ]
+    step_of_row = iota((PLANES, LOCAL), 0)
     fits = jnp.ones((1, 1), F32)
-    injected, arrived = [], []
-    for up in (True, False):
+    heights = {}
+    for way in range(2):
         height = jnp.zeros((1, 1), F32)
-        end = jnp.full((known, 1), -1.0, F32)
-        held = jnp.full((known, 1), -1.0, F32)
-        mine_in = jnp.full((known, 1), -1.0, F32)
-        mine_arrived = jnp.full((known, 1), -1.0, F32)
         for step in range(PLANES - 1):
-            z = step if up else PLANES - 1 - step
-            reach = top[:, z * LOCAL : (z + 1) * LOCAL]
-            if not up:
-                reach = (PLANES - 1) - low[:, z * LOCAL : (z + 1) * LOCAL]
-            fresh = (reach > step).astype(F32)
-            kinds = (reach == kind).astype(F32) * fresh
-            of_kind = jnp.dot(kinds.astype(BF16), before_lane, preferred_element_type=F32)
-            earlier = jnp.dot(
-                before_kind,
-                jnp.broadcast_to(jnp.sum(kinds, axis=1, keepdims=True), (8, HD)).astype(BF16),
-                preferred_element_type=F32,
-            )[:, 0:1]
-            fresh_rank = jnp.sum(kinds * (of_kind + earlier), axis=0, keepdims=True)
-            load = jnp.sum((end > step).astype(F32), axis=0, keepdims=True) + jnp.sum(
-                fresh, axis=1, keepdims=True
+            over = (stacked[way] > step) & (step_of_row <= step)
+            load = jnp.sum(
+                jnp.sum(over.astype(F32), axis=1, keepdims=True), axis=0, keepdims=True
             )
             height = jnp.maximum(height, load)
-            free = ((end <= step) & (slot_column < height)).astype(F32)
-            free_rank = jnp.dot(
-                after_row, jnp.broadcast_to(free, (known, HD)).astype(BF16), preferred_element_type=F32
-            )[:, 0:1]
-            pair = (free_rank == fresh_rank) & (free > 0.5) & (fresh > 0.5)
-            code = jnp.sum(jnp.where(pair, 1.0 + lane + LOCAL * reach, 0.0), axis=1, keepdims=True)
-            taken = code > 0.5
-            new_end = jnp.floor((code - 1.0) / LOCAL)
-            new_block = code - 1.0 - LOCAL * new_end
-            inject = jnp.where(taken, new_block, -1.0)
-            held = jnp.where(taken, z * LOCAL + new_block, jnp.where(end <= step, -1.0, held))
-            end = jnp.where(taken, new_end, end)
+            heights[way, step] = height
             fits = fits * (load <= caps[min(step, 3)]).astype(F32)
-            if step == PLANES - 2:
-                lowest = jnp.min(
-                    jnp.where(end > step, slot_column, known), axis=0, keepdims=True
-                )
-                fits = fits * (lowest >= left_out).astype(F32)
-            mine_in = jnp.where(my_z == z, inject, mine_in)
-            mine_arrived = jnp.where(my_z == (z + 1 if up else z - 1), held, mine_arrived)
-        injected.append(mine_in)
-        arrived.append(mine_arrived)
-    diagonal = iota((known, known), 0) == iota((known, known), 1)
-
-    def as_row(column):
-        return jnp.sum(jnp.where(diagonal, column, 0.0), axis=0, keepdims=True)
-
-    in_up, in_down = as_row(injected[0]), as_row(injected[1])
-    at_up, at_down = as_row(arrived[0]), as_row(arrived[1])
+
+    kinds = jnp.concatenate(
+        [
+            ((reaches[turn] == kind) & (reaches[turn] > turn[1])).astype(F32)
+            for turn in turns
+        ],
+        axis=0,
+    )
+    many = 8 * len(turns)
+    before_lane = (iota((LOCAL, LOCAL), 0) < iota((LOCAL, LOCAL), 1)).astype(BF16)
+    turn_row, turn_column = (
+        jnp.floor(iota((many, many), 0) / 8),
+        jnp.floor(iota((many, many), 1) / 8),
+    )
+    before_kind = (
+        (turn_row == turn_column) & (iota((many, many), 1) < iota((many, many), 0))
+    ).astype(BF16)
+    of_kind = jnp.dot(kinds.astype(BF16), before_lane, preferred_element_type=F32)
+    earlier = jnp.dot(
+        before_kind,
+        jnp.broadcast_to(jnp.sum(kinds, axis=1, keepdims=True), (many, HD)).astype(BF16),
+        preferred_element_type=F32,
+    )[:, 0:1]
+    ranked = kinds * (of_kind + earlier)
+    ranks = {
+        turn: jnp.sum(ranked[8 * i : 8 * i + 8], axis=0, keepdims=True)
+        for i, turn in enumerate(turns)
+    }
+
+    eye = (iota((LOCAL, LOCAL), 0) == iota((LOCAL, LOCAL), 1)).astype(BF16)
+
+    def as_columns(rows):
+        return lax.dot_general(
+            eye, rows.astype(BF16), (((1,), (1,)), ((), ())), preferred_element_type=F32
+        )
+
+    reach_columns = [as_columns(rows) for rows in stacked]
+    rank_columns = as_columns(
+        jnp.concatenate([ranks[turn] for turn in turns] + [ranks[turns[0]]] * 2, axis=0)
+    )
+    place_column = iota((LOCAL, 1), 0)
+    after_lane = (iota((known, known), 0) > iota((known, known), 1)).astype(BF16)
+    slot_row = iota((1, known), 1)
+    nothing = jnp.full((1, known), -1.0, F32)
+    ends, helds = [nothing, nothing], [nothing, nothing]
+    injected, arrived = [nothing, nothing], [nothing, nothing]
+    for i, (way, step) in enumerate(turns):
+        z = plane(way, step)
+        reach = reach_columns[way][:, step : step + 1]
+        rank = jnp.where(reach > step, rank_columns[:, i : i + 1], -2.0)
+        end = ends[way]
+        free = (end <= step) & (slot_row < heights[way, step])
+        free_rank = jnp.dot(
+            jnp.broadcast_to(free.astype(F32), (8, known)).astype(BF16),
+            after_lane,
+            preferred_element_type=F32,
+        )[0:1]
+        pair = rank == jnp.where(free, free_rank, -1.0)
+        code = jnp.sum(
+            jnp.where(pair, 1.0 + place_column + LOCAL * reach, 0.0), axis=0, keepdims=True
+        )
+        taken = code > 0.5
+        new_end = jnp.floor((code - 1.0) / LOCAL)
+        new_block = code - 1.0 - LOCAL * new_end
+        helds[way] = jnp.where(
+            taken, z * LOCAL + new_block, jnp.where(end <= step, -1.0, helds[way])
+        )
+        ends[way] = jnp.where(taken, new_end, end)
+        injected[way] = jnp.where(my_z == z, jnp.where(taken, new_block, -1.0), injected[way])
+        arrived[way] = jnp.where(my_z == plane(way, step + 1), helds[way], arrived[way])
+        if step == PLANES - 2:
+            lowest = jnp.min(
+                jnp.where(ends[way] > step, slot_row, known), axis=1, keepdims=True
+            )
+            fits = fits * (lowest >= left_out).astype(F32)
+    in_up, in_down = injected
+    at_up, at_down = arrived
     rows = iota((8, HD), 0)
     out = jnp.where(rows == 4, fits, 0.0)
     for i in range(known // HD):
@@ -600,9 +644,8 @@
     far = jnp.maximum(z, PLANES - 1 - z)
     far = lag_at(far) - floor_at(far - 1)
     pieces = 2 * HEADS_HERE
-    every = max(1, (steps - 12) // (pieces + 2))
     pass_step = 5
-    first_piece = steps - 4 - every * pieces
+    early, every, first_piece = 3, 2, groups + 6
 
     def step_body(k, carry):
         for chunk in range(1, CHUNKS):
@@ -645,13 +688,19 @@
         since = k - first_piece
         piece = jnp.maximum(since, 0) // every
 
-        @pl.when((since >= 0) & (since % every == 0) & (piece < pieces))
+        @pl.when((since >= 0) & (since % every == 0) & (piece < early))
         def _():
             window_piece(piece // 2, piece % 2)
 
         return carry
 
     lax.fori_loop(0, steps, step_body, 0)
+
+    def late_piece(piece, carry):
+        window_piece(piece // 2, piece % 2)
+        return carry
+
+    lax.fori_loop(early, pieces, late_piece, 0)
 
     for c in range(CHUNKS):
         for r in range(1, 8):

time: 111 us -> 107 us (0.964)
  Pallas kernels: 108 us -> 105 us
    pallas_call x1, Pallas kernels: 108 us -> 105 us  [attend(): pl.pallas_call(functools.partial(attend_kernel, tier), out_shape=[jax.Sha...]
where the time goes in v4:
time: 107 us
  Pallas kernels  105 us (98%)
  local copies, waits for them, and re-layouts  1.42 us (1%)
    pallas_call x1, Pallas kernels, attend(): pl.pallas_call(functools.partial(attend_kernel, tier), out_shape=[jax.Sha...  105 us

profile of v4, /device:TPU:1, one launch (start us, length us, event | category | flops | bytes accessed | tf_op | source)
XLA Modules:
  0.0 107.0 jit_solution(12431683441991778236)
XLA Ops:
  0.0 0.0 copy-start.5
  0.0 0.0 copy-start.6
  0.0 0.0 copy-start.7
  0.0 0.7 copy-done.5
  0.7 0.0 copy-done.6
  0.7 0.0 copy-done.7
  0.7 0.0 copy-start
  0.7 0.0 copy-start.1
  0.7 0.0 copy-start.2
  0.7 0.0 copy-start.3
  0.7 0.0 copy-start.4
  0.7 104.6 %attend_112.1 = (bf16[256,512]{1,0:T(8,128)(2,1)S(1)}, s32[1]{0:T(128)}) custom-call(s32[2,4]{1,0:T(2,128)S(1)} %copy-done.6, f32[1,4]{1,0:T(1,128)S(1)} %bitcast.5, f32[1,512]{1,0:T(1,128)S(1)} %bitcast.3, bf16[256,512]{1,0:T(8,128)(2,1)} %refs_3_.1, bf16[256,512]{1,0:T(8,128)(2,1)} %refs_4_.1, bf16[256,512]{1,0:T(8,128)(2,1)} %refs_5_.1, ...), custom_call_target="tpu_custom_call" | custom-call | tf_op jit(solution)/shard_map/attend_112/pallas_call | solution.py:835
  106.0 0.0 copy-done
  106.0 0.0 copy-done.1
  106.0 0.0 copy-done.2
  106.0 0.0 copy-done.3
  106.0 0.0 copy-done.4
  106.0 0.2 conditional.1
  106.3 0.7 copy.14
Async XLA Ops:
  0.0 0.7 copy-start.5
  0.0 0.7 copy-start.6
  0.0 0.7 copy-start.7
  0.7 105.3 %copy-start = (bf16[8,64,512]{2,1,0:T(8,128)(2,1)S(1)}, bf16[8,64,512]{2,1,0:T(8,128)(2,1)}, u32[]{:S(2)}) copy-start(bf16[8,64,512]{2,1,0:T(8,128)(2,1)} %refs_6_.1) | copy-start | bytes 1572868
  0.7 105.3 %copy-start.1 = (bf16[8,64,512]{2,1,0:T(8,128)(2,1)S(1)}, bf16[8,64,512]{2,1,0:T(8,128)(2,1)}, u32[]{:S(2)}) copy-start(bf16[8,64,512]{2,1,0:T(8,128)(2,1)} %refs_7_.1) | copy-start | bytes 1572868
  0.7 105.3 %copy-start.2 = (bf16[256,512]{1,0:T(8,128)(2,1)S(1)}, bf16[256,512]{1,0:T(8,128)(2,1)}, u32[]{:S(2)}) copy-start(bf16[256,512]{1,0:T(8,128)(2,1)} %refs_3_.1) | copy-start | bytes 786436
  0.7 105.3 %copy-start.3 = (bf16[256,512]{1,0:T(8,128)(2,1)S(1)}, bf16[256,512]{1,0:T(8,128)(2,1)}, u32[]{:S(2)}) copy-start(bf16[256,512]{1,0:T(8,128)(2,1)} %refs_4_.1) | copy-start | bytes 786436
  0.7 105.3 %copy-start.4 = (bf16[256,512]{1,0:T(8,128)(2,1)S(1)}, bf16[256,512]{1,0:T(8,128)(2,1)}, u32[]{:S(2)}) copy-start(bf16[256,512]{1,0:T(8,128)(2,1)} %refs_5_.1) | copy-start | bytes 786436

commit v5 on v4

--- a/solution.py
+++ b/solution.py
@@ -28,7 +28,7 @@
 ROWS = BLK // CHUNKS
 SCALE = 1.0 / math.sqrt(HD)
 
-SHORT = ((56, 88, 104, 112), 8, (3, 7, 10, 11), 16, 128)
+SHORT = ((56, 80, 104, 112), 8, (3, 7, 10, 11), 16, 128)
 LONG = ((64, 128, 192, 256), 16, (2, 4, 6, 8), 0, 256)
 REACHES = (7, 1, 2, 3, 4, 5, 6)
 

time: 107 us -> 106 us (level)
  no operation moved by 1% of the time
where the time goes in v5:
time: 106 us
  Pallas kernels  104 us (98%)
  local copies, waits for them, and re-layouts  1.42 us (1%)
    pallas_call x1, Pallas kernels, attend(): pl.pallas_call(functools.partial(attend_kernel, tier), out_shape=[jax.Sha...  104 us

profile of v5, /device:TPU:1, one launch (start us, length us, event | category | flops | bytes accessed | tf_op | source)
XLA Modules:
  0.0 106.0 jit_solution(16312171417716647080)
XLA Ops:
  0.0 0.0 copy-start.5
  0.0 0.0 copy-start.6
  0.0 0.0 copy-start.7
  0.0 0.7 copy-done.5
  0.7 0.0 copy-done.6
  0.7 0.0 copy-done.7
  0.7 0.0 copy-start
  0.7 0.0 copy-start.1
  0.7 0.0 copy-start.2
  0.7 0.0 copy-start.3
  0.7 0.0 copy-start.4
  0.7 103.7 %attend_112.1 = (bf16[256,512]{1,0:T(8,128)(2,1)S(1)}, s32[1]{0:T(128)}) custom-call(s32[2,4]{1,0:T(2,128)S(1)} %copy-done.6, f32[1,4]{1,0:T(1,128)S(1)} %bitcast.5, f32[1,512]{1,0:T(1,128)S(1)} %bitcast.3, bf16[256,512]{1,0:T(8,128)(2,1)} %refs_3_.1, bf16[256,512]{1,0:T(8,128)(2,1)} %refs_4_.1, bf16[256,512]{1,0:T(8,128)(2,1)} %refs_5_.1, ...), custom_call_target="tpu_custom_call" | custom-call | tf_op jit(solution)/shard_map/attend_112/pallas_call | solution.py:835
  105.0 0.0 copy-done
  105.0 0.0 copy-done.1
  105.1 0.0 copy-done.2
  105.1 0.0 copy-done.3
  105.1 0.0 copy-done.4
  105.1 0.2 conditional.1
  105.3 0.7 copy.14
Async XLA Ops:
  0.0 0.7 copy-start.5
  0.0 0.7 copy-start.6
  0.0 0.7 copy-start.7
  0.7 104.3 %copy-start = (bf16[8,64,512]{2,1,0:T(8,128)(2,1)S(1)}, bf16[8,64,512]{2,1,0:T(8,128)(2,1)}, u32[]{:S(2)}) copy-start(bf16[8,64,512]{2,1,0:T(8,128)(2,1)} %refs_6_.1) | copy-start | bytes 1572868
  0.7 104.3 %copy-start.1 = (bf16[8,64,512]{2,1,0:T(8,128)(2,1)S(1)}, bf16[8,64,512]{2,1,0:T(8,128)(2,1)}, u32[]{:S(2)}) copy-start(bf16[8,64,512]{2,1,0:T(8,128)(2,1)} %refs_7_.1) | copy-start | bytes 1572868
  0.7 104.4 %copy-start.2 = (bf16[256,512]{1,0:T(8,128)(2,1)S(1)}, bf16[256,512]{1,0:T(8,128)(2,1)}, u32[]{:S(2)}) copy-start(bf16[256,512]{1,0:T(8,128)(2,1)} %refs_3_.1) | copy-start | bytes 786436
  0.7 104.4 %copy-start.3 = (bf16[256,512]{1,0:T(8,128)(2,1)S(1)}, bf16[256,512]{1,0:T(8,128)(2,1)}, u32[]{:S(2)}) copy-start(bf16[256,512]{1,0:T(8,128)(2,1)} %refs_4_.1) | copy-start | bytes 786436
  0.7 104.4 %copy-start.4 = (bf16[256,512]{1,0:T(8,128)(2,1)S(1)}, bf16[256,512]{1,0:T(8,128)(2,1)}, u32[]{:S(2)}) copy-start(bf16[256,512]{1,0:T(8,128)(2,1)} %refs_5_.1) | copy-start | bytes 786436

commit v6 on v5

--- a/solution.py
+++ b/solution.py
@@ -248,7 +248,7 @@
     def mem_peer(r):
         return {"mem": (mem + r) % 8}
 
-    above, below = {"ctx": me + PLANE}, {"ctx": me - PLANE}
+    above, below = on_line(1), on_line(PLANES - 1)
     loads = [
         pltpu.make_async_copy(k_ref, near_k.at[pl.ds(2 * TOK, TOK)], own_sem.at[0]),
         pltpu.make_async_copy(v_ref, near_v.at[pl.ds(2 * TOK, TOK)], own_sem.at[1]),

time: 106 us -> 106 us (level)
  no operation moved by 1% of the time
where the time goes in v6:
time: 106 us
  Pallas kernels  104 us (98%)
  local copies, waits for them, and re-layouts  1.42 us (1%)
    pallas_call x1, Pallas kernels, attend(): pl.pallas_call(functools.partial(attend_kernel, tier), out_shape=[jax.Sha...  104 us

profile of v6, /device:TPU:1, one launch (start us, length us, event | category | flops | bytes accessed | tf_op | source)
XLA Modules:
  0.0 106.2 jit_solution(4640830384529956196)
XLA Ops:
  0.0 0.0 copy-start.5
  0.0 0.0 copy-start.6
  0.0 0.0 copy-start.7
  0.0 0.7 copy-done.5
  0.7 0.0 copy-done.6
  0.7 0.0 copy-done.7
  0.7 0.0 copy-start
  0.7 0.0 copy-start.1
  0.7 0.0 copy-start.2
  0.7 0.0 copy-start.3
  0.7 0.0 copy-start.4
  0.7 103.8 %attend_112.1 = (bf16[256,512]{1,0:T(8,128)(2,1)S(1)}, s32[1]{0:T(128)}) custom-call(s32[2,4]{1,0:T(2,128)S(1)} %copy-done.6, f32[1,4]{1,0:T(1,128)S(1)} %bitcast.5, f32[1,512]{1,0:T(1,128)S(1)} %bitcast.3, bf16[256,512]{1,0:T(8,128)(2,1)} %refs_3_.1, bf16[256,512]{1,0:T(8,128)(2,1)} %refs_4_.1, bf16[256,512]{1,0:T(8,128)(2,1)} %refs_5_.1, ...), custom_call_target="tpu_custom_call" | custom-call | tf_op jit(solution)/shard_map/attend_112/pallas_call | solution.py:835
  105.2 0.0 copy-done
  105.2 0.0 copy-done.1
  105.2 0.0 copy-done.2
  105.2 0.0 copy-done.3
  105.2 0.0 copy-done.4
  105.2 0.2 conditional.1
  105.4 0.7 copy.14
Async XLA Ops:
  0.0 0.7 copy-start.5
  0.0 0.7 copy-start.6
  0.0 0.7 copy-start.7
  0.7 104.5 %copy-start = (bf16[8,64,512]{2,1,0:T(8,128)(2,1)S(1)}, bf16[8,64,512]{2,1,0:T(8,128)(2,1)}, u32[]{:S(2)}) copy-start(bf16[8,64,512]{2,1,0:T(8,128)(2,1)} %refs_6_.1) | copy-start | bytes 1572868
  0.7 104.5 %copy-start.1 = (bf16[8,64,512]{2,1,0:T(8,128)(2,1)S(1)}, bf16[8,64,512]{2,1,0:T(8,128)(2,1)}, u32[]{:S(2)}) copy-start(bf16[8,64,512]{2,1,0:T(8,128)(2,1)} %refs_7_.1) | copy-start | bytes 1572868
  0.7 104.5 %copy-start.2 = (bf16[256,512]{1,0:T(8,128)(2,1)S(1)}, bf16[256,512]{1,0:T(8,128)(2,1)}, u32[]{:S(2)}) copy-start(bf16[256,512]{1,0:T(8,128)(2,1)} %refs_3_.1) | copy-start | bytes 786436
  0.7 104.5 %copy-start.3 = (bf16[256,512]{1,0:T(8,128)(2,1)S(1)}, bf16[256,512]{1,0:T(8,128)(2,1)}, u32[]{:S(2)}) copy-start(bf16[256,512]{1,0:T(8,128)(2,1)} %refs_4_.1) | copy-start | bytes 786436
  0.7 104.5 %copy-start.4 = (bf16[256,512]{1,0:T(8,128)(2,1)S(1)}, bf16[256,512]{1,0:T(8,128)(2,1)}, u32[]{:S(2)}) copy-start(bf16[256,512]{1,0:T(8,128)(2,1)} %refs_5_.1) | copy-start | bytes 786436
